TPU v7x, 256 devices: a whole 4x4x8 slice. The times are simulated.
256 devices in a mesh: space: 32 (over x, y, core), mem: 8 (over z).
Axes of the slice: x: 4, y: 4, z: 8, core: 2. Of those that a mesh axis runs over, the one named last changes fastest.
Arguments:
- fields: bfloat16 [64, 64, 64, 384], P('mem', None, 'space'), may hold values from -6 to 6
- w_qkv: bfloat16 [9, 192, 64], replicated, may hold values from -1 to 1
- w_out: bfloat16 [9, 64, 64], replicated, may hold values from -0.25 to 0.25
Outputs:
- mixed: bfloat16 [64, 64, 64, 384], P('mem', None, 'space')
All inputs are finite; a program needn't handle non-finite values.
Results may differ from a plain program's by a relative error of at most 0.007.
Values may be sent and summed in bfloat16 or wider, within the bound.
No kernel may reach another device: no remote copies, remote signals or barrier semaphores. Data moves between devices by JAX's collectives and lax.ppermute only.
A program may use at most 64 MiB of HBM per device.

v0:
```python
import math

import jax
import jax.numpy as jnp
from jax import lax
from jax.sharding import PartitionSpec as P

HEADS = 8


def with_halo(cells, sides, width):
    for axis, dim in sides:
        count = lax.axis_size(axis)
        ends = count - 1
        head = lax.slice_in_dim(cells, 0, width, axis=dim)
        tail = lax.slice_in_dim(cells, cells.shape[dim] - width, cells.shape[dim], axis=dim)
        cells = jnp.concatenate(
            [
                lax.ppermute(tail, axis, [(i, (i + 1) % count) for i in range(ends)]),
                cells,
                lax.ppermute(head, axis, [((i + 1) % count, i) for i in range(ends)]),
            ],
            axis=dim,
        )
    return cells


def pad_longitude(field):
    return jnp.pad(field, ((0, 0), (0, 0), (0, 0), (1, 1)))


def convolve(padded, weights, lat_rows, lon_cols):
    summed = jnp.zeros((padded.shape[0], weights.shape[1], lat_rows, lon_cols), jnp.float32)
    for lat_shift in range(3):
        for lon_shift in range(3):
            shifted = padded[
                :, :, lat_shift : lat_shift + lat_rows, lon_shift : lon_shift + lon_cols
            ]
            summed = summed + jnp.einsum(
                "oc,mcyx->moyx",
                weights[3 * lat_shift + lon_shift],
                shifted,
                preferred_element_type=jnp.float32,
            )
    return summed


def local(fields, w_qkv, w_out):
    members_here, channels, lat_rows, lon_cols = fields.shape
    padded_field = pad_longitude(with_halo(fields, (("space", 2),), 1))

    def project(which_map):
        return convolve(
            padded_field,
            w_qkv[:, which_map * channels : (which_map + 1) * channels],
            lat_rows,
            lon_cols,
        ).astype(jnp.bfloat16)

    queries = project(0)
    key_maps = project(1)
    head_dim = channels // HEADS
    score_scale = 1.0 / math.sqrt(head_dim * lat_rows * lax.axis_size("space") * lon_cols)
    group_count = lax.axis_size("mem")
    all_members = members_here * group_count
    local_heads = HEADS // group_count
    queries_h, keys_h = (
        lax.all_to_all(queries, "mem", split_axis=1, concat_axis=0, tiled=True),
        lax.all_to_all(key_maps, "mem", split_axis=1, concat_axis=0, tiled=True),
    )
    head_shape = (all_members, local_heads, head_dim, lat_rows, lon_cols)
    partial_scores = jnp.einsum(
        "ihdyx,jhdyx->hij",
        queries_h.reshape(head_shape),
        keys_h.reshape(head_shape),
        preferred_element_type=jnp.float32,
    )
    scores = lax.psum(partial_scores * score_scale, "space")
    attn = jax.nn.softmax(scores, axis=-1).astype(jnp.bfloat16)
    values = project(2)
    value_rows = lax.all_to_all(values, "mem", split_axis=1, concat_axis=0, tiled=True)
    row_count = value_rows.shape[2]
    value_heads = value_rows.reshape(all_members, local_heads, head_dim, row_count, lon_cols)
    blended = jnp.einsum("hij,jhdyx->ihdyx", attn, value_heads, preferred_element_type=jnp.float32)
    blended = blended.astype(jnp.bfloat16).reshape(
        all_members, local_heads * head_dim, row_count, lon_cols
    )
    attended = lax.all_to_all(blended, "mem", split_axis=0, concat_axis=1, tiled=True)
    padded_attended = pad_longitude(with_halo(attended, (("space", 2),), 1))
    update = convolve(padded_attended, w_out, lat_rows, lon_cols)
    return (fields.astype(jnp.float32) + update).astype(jnp.bfloat16)


def solution(mesh):
    return jax.shard_map(
        local,
        mesh=mesh,
        in_specs=(P("mem", None, "space", None), P(), P()),
        out_specs=P("mem", None, "space", None),
        check_vma=False,
    )
```

profile of v0, /device:TPU:1, one launch (start us, length us, event | category | flops | bytes accessed | tf_op | source)
XLA Modules:
  0.0 257.8 jit_solution(10657527072053751731)
XLA Ops:
  1.5 4.6 %collective-permute-start = (bf16[8,64,1,384]{3,1,2,0:T(8,128)(2,1)S(1)}, bf16[8,64,1,384]{3,1,2,0:T(8,128)(2,1)S(1)}, u32[]{:S(2)}, u32[]{:S(2)}) collective-permute-start(bf16[8,64,1,384]{3,1,2,0:T(8,128)(2,1)S(1)} %get-tuple-element.7), channel_id=1, source_target_pairs={{0,8},{8,16},{16,24},{24,32},{32,40},{40,48},{48,56},{56,64},{64,7... | collective-permute-start | bytes 1179656 | tf_op jit(solution)/shard_map/ppermute | solution.py:19
  6.1 1.9 collective-permute-start.1
  8.4 1.6 fusion.97
  10.0 1.6 fusion.85
  11.6 3.6 %collective-permute-done.1 = bf16[8,64,1,384]{3,1,2,0:T(8,128)(2,1)S(1)} collective-permute-done((bf16[8,64,1,384]{3,1,2,0:T(8,128)(2,1)S(1)}, bf16[8,64,1,384]{3,1,2,0:T(8,128)(2,1)S(1)}, u32[]{:S(2)}, u32[]{:S(2)}) %collective-permute-start.1) | collective-permute-done | bytes 393248 | tf_op jit(solution)/shard_map/ppermute | solution.py:21
  18.5 1.7 fusion.53
  20.2 1.6 fusion.59
  21.8 1.6 fusion.65
  23.4 1.7 fusion.71
  25.1 1.6 fusion.77
  28.4 1.7 copy.73
  30.1 8.2 %all-to-all-start.1 = ((bf16[8,64,2,384]{3,2,0,1:T(2,128)(2,1)}), bf16[8,64,2,384]{3,2,0,1:T(2,128)(2,1)}, u32[]{:S(2)}, u32[]{:S(2)}) async-start(bf16[8,64,2,384]{3,2,0,1:T(2,128)(2,1)} %copy.73), calls=%async_computation.1 | async-start | bytes 1572864 | tf_op jit(solution)/shard_map/all_to_all | solution.py:68
  38.3 1.6 fusion.101
  41.5 3.2 %fusion.12 = bf16[8,64,2,384]{3,1,2,0:T(8,128)(2,1)S(1)} fusion(f32[8,2,384,64]{2,3,1,0:T(8,128)S(1)} %fusion.93, f32[8,2,384,64]{2,3,1,0:T(8,128)S(1)} %copy-done.4, f32[8,2,384,64]{2,3,1,0:T(8,128)S(1)} %copy-done.5, f32[8,2,384,64]{2,3,1,0:T(8,128)S(1)} %copy-done.3, f32[8,2,384,64]{2,3,1,0:T(8,128)} %fusion.65, f32[8,2,384,64]{2,3,1,0:T(8,128)} %fusion.71, ...), kind=kOutput, calls=%fused_computation.22 | convolution fusion | flops 53870592 | bytes 14172160 | tf_op jit(solution)/shard_map/oc,mcyx->moyx/dot_general | solution.py:39
  44.7 1.8 copy.85
  46.5 2.3 fusion.89
  48.7 2.3 fusion.49
  51.0 2.4 fusion.55
  53.3 2.2 fusion.61
  55.6 1.5 all-to-all-done.1
  57.1 5.2 %all-to-all-start.2 = ((bf16[8,64,2,384]{3,2,0,1:T(2,128)(2,1)}), bf16[8,64,2,384]{3,2,0,1:T(2,128)(2,1)}, u32[]{:S(2)}, u32[]{:S(2)}) async-start(bf16[8,64,2,384]{3,2,0,1:T(2,128)(2,1)} %copy.85), calls=%async_computation.2 | async-start | bytes 1572864 | tf_op jit(solution)/shard_map/all_to_all | solution.py:69
  66.4 2.3 fusion.10
  68.7 1.7 copy.61
  70.4 11.8 %all-to-all-done.2 = bf16[8,64,2,384]{3,2,0,1:T(2,128)(2,1)} async-done(((bf16[8,64,2,384]{3,2,0,1:T(2,128)(2,1)}), bf16[8,64,2,384]{3,2,0,1:T(2,128)(2,1)}, u32[]{:S(2)}, u32[]{:S(2)}) %all-to-all-start.2) | async-done | bytes 786464 | tf_op jit(solution)/shard_map/all_to_all | solution.py:69
  82.1 3.5 %all-to-all-start = ((bf16[8,64,2,384]{3,2,0,1:T(2,128)(2,1)}), bf16[8,64,2,384]{3,2,0,1:T(2,128)(2,1)S(1)}, u32[]{:S(2)}, u32[]{:S(2)}) async-start(bf16[8,64,2,384]{3,2,0,1:T(2,128)(2,1)} %copy.61), calls=%async_computation | async-start | bytes 1572864 | tf_op jit(solution)/shard_map/all_to_all | solution.py:81
  85.7 1.7 fusion.9
  87.4 124.0 %psum.7 = f32[1,64,64]{2,1,0:T(8,128)S(1)} all-reduce(f32[1,64,64]{2,1,0:T(8,128)S(1)} %fusion.9), channel_id=1, replica_groups=mesh['space'=32,'mem'=8] {'space'}, use_global_device_ids=true, to_apply=%region_0.1 | all-reduce | flops 4096 | bytes 32768 | tf_op jit(solution)/shard_map/psum | solution.py:78
  213.0 22.3 %all_to_all.63 = bf16[64,8,2,384]{3,2,1,0:T(2,128)(2,1)S(1)} all-to-all(bf16[64,8,2,384]{3,2,1,0:T(2,128)(2,1)S(1)} %copy.87), channel_id=1, replica_groups=mesh['space'=32,'mem'=8] {'mem'}, dimensions={0} | all-to-all | bytes 1572864 | tf_op jit(solution)/shard_map/all_to_all | solution.py:88
  235.6 5.8 %collective-permute-start.2 = (bf16[8,64,1,384]{3,1,2,0:T(8,128)(2,1)S(1)}, bf16[8,64,1,384]{3,1,2,0:T(8,128)(2,1)S(1)}, u32[]{:S(2)}, u32[]{:S(2)}) collective-permute-start(bf16[8,64,1,384]{3,1,2,0:T(8,128)(2,1)S(1)} %get-tuple-element.5), channel_id=1, source_target_pairs={{0,8},{8,16},{16,24},{24,32},{32,40},{40,48},{48,56},{56,64},{64,7... | collective-permute-start | bytes 1179656 | tf_op jit(solution)/shard_map/ppermute | solution.py:19
  241.4 5.3 %collective-permute-start.3 = (bf16[8,64,1,384]{3,1,2,0:T(8,128)(2,1)S(1)}, bf16[8,64,1,384]{3,1,2,0:T(8,128)(2,1)S(1)}, u32[]{:S(2)}, u32[]{:S(2)}) collective-permute-start(bf16[8,64,1,384]{3,1,2,0:T(8,128)(2,1)S(1)} %get-tuple-element.6), channel_id=1, source_target_pairs={{8,0},{16,8},{24,16},{32,24},{40,32},{48,40},{56,48},{64,56},{72,6... | collective-permute-start | bytes 1179656 | tf_op jit(solution)/shard_map/ppermute | solution.py:21
  247.0 3.5 %collective-permute-done.3 = bf16[8,64,1,384]{3,1,2,0:T(8,128)(2,1)S(1)} collective-permute-done((bf16[8,64,1,384]{3,1,2,0:T(8,128)(2,1)S(1)}, bf16[8,64,1,384]{3,1,2,0:T(8,128)(2,1)S(1)}, u32[]{:S(2)}, u32[]{:S(2)}) %collective-permute-start.3) | collective-permute-done | bytes 393248 | tf_op jit(solution)/shard_map/ppermute | solution.py:21
  256.1 1.7 copy.89
  (61 shorter events, 20.1 us)
Async XLA Ops:
  0.0 8.0 %copy-start = (bf16[8,64,2,384]{3,2,1,0:T(2,128)(2,1)S(1)}, bf16[8,64,2,384]{3,2,1,0:T(2,128)(2,1)}, u32[]{:S(2)}) copy-start(bf16[8,64,2,384]{3,2,1,0:T(2,128)(2,1)} %param.3) | copy-start | bytes 2359300
  0.0 8.0 %copy-start.11 = (bf16[9,192,64]{1,2,0:T(8,128)(2,1)S(1)}, bf16[9,192,64]{1,2,0:T(8,128)(2,1)}, u32[]{:S(2)}) copy-start(bf16[9,192,64]{1,2,0:T(8,128)(2,1)} %param.4) | copy-start | bytes 663556
  1.5 10.1 %collective-permute-start = (bf16[8,64,1,384]{3,1,2,0:T(8,128)(2,1)S(1)}, bf16[8,64,1,384]{3,1,2,0:T(8,128)(2,1)S(1)}, u32[]{:S(2)}, u32[]{:S(2)}) collective-permute-start(bf16[8,64,1,384]{3,1,2,0:T(8,128)(2,1)S(1)} %get-tuple-element.7), channel_id=1, source_target_pairs={{0,8},{8,16},{16,24},{24,32},{32,40},{40,48},{48,56},{56,64},{64,7... | collective-permute-start | bytes 1179656 | tf_op jit(solution)/shard_map/ppermute | solution.py:19
  6.1 9.1 %collective-permute-start.1 = (bf16[8,64,1,384]{3,1,2,0:T(8,128)(2,1)S(1)}, bf16[8,64,1,384]{3,1,2,0:T(8,128)(2,1)S(1)}, u32[]{:S(2)}, u32[]{:S(2)}) collective-permute-start(bf16[8,64,1,384]{3,1,2,0:T(8,128)(2,1)S(1)} %get-tuple-element.8), channel_id=1, source_target_pairs={{8,0},{16,8},{24,16},{32,24},{40,32},{48,40},{56,48},{64,56},{72,6... | collective-permute-start | bytes 1179656 | tf_op jit(solution)/shard_map/ppermute | solution.py:21
  11.6 15.5 %copy-start.9 = (bf16[8,64,1,384]{3,1,2,0:T(8,128)(2,1)}, bf16[8,64,1,384]{3,1,2,0:T(8,128)(2,1)S(1)}, u32[]{:S(2)}) copy-start(bf16[8,64,1,384]{3,1,2,0:T(8,128)(2,1)S(1)} %collective-permute-done) | copy-start | bytes 1179652
  30.1 27.0 %all-to-all-start.1 = ((bf16[8,64,2,384]{3,2,0,1:T(2,128)(2,1)}), bf16[8,64,2,384]{3,2,0,1:T(2,128)(2,1)}, u32[]{:S(2)}, u32[]{:S(2)}) async-start(bf16[8,64,2,384]{3,2,0,1:T(2,128)(2,1)} %copy.73), calls=%async_computation.1 | async-start | bytes 1572864 | tf_op jit(solution)/shard_map/all_to_all | solution.py:68
  38.3 3.0 %copy-start.4 = (f32[8,2,384,64]{2,3,1,0:T(8,128)S(1)}, f32[8,2,384,64]{2,3,1,0:T(8,128)}, u32[]{:S(2)}) copy-start(f32[8,2,384,64]{2,3,1,0:T(8,128)} %fusion.53) | copy-start | bytes 4718596
  38.3 3.0 %copy-start.5 = (f32[8,2,384,64]{2,3,1,0:T(8,128)S(1)}, f32[8,2,384,64]{2,3,1,0:T(8,128)}, u32[]{:S(2)}) copy-start(f32[8,2,384,64]{2,3,1,0:T(8,128)} %fusion.59) | copy-start | bytes 4718596
  39.9 1.5 copy-start.3
  44.7 1.8 copy-start.10
  57.1 25.1 %all-to-all-start.2 = ((bf16[8,64,2,384]{3,2,0,1:T(2,128)(2,1)}), bf16[8,64,2,384]{3,2,0,1:T(2,128)(2,1)}, u32[]{:S(2)}, u32[]{:S(2)}) async-start(bf16[8,64,2,384]{3,2,0,1:T(2,128)(2,1)} %copy.85), calls=%async_computation.2 | async-start | bytes 1572864 | tf_op jit(solution)/shard_map/all_to_all | solution.py:69
  62.2 3.8 %copy-start.8 = (f32[8,2,384,64]{2,3,1,0:T(8,128)S(1)}, f32[8,2,384,64]{2,3,1,0:T(8,128)}, u32[]{:S(2)}) copy-start(f32[8,2,384,64]{2,3,1,0:T(8,128)} %fusion.61) | copy-start | bytes 4718596
  63.5 2.6 %copy-start.6 = (f32[8,2,384,64]{2,3,1,0:T(8,128)S(1)}, f32[8,2,384,64]{2,3,1,0:T(8,128)}, u32[]{:S(2)}) copy-start(f32[8,2,384,64]{2,3,1,0:T(8,128)} %fusion.49) | copy-start | bytes 4718596
  63.5 2.6 %copy-start.7 = (f32[8,2,384,64]{2,3,1,0:T(8,128)S(1)}, f32[8,2,384,64]{2,3,1,0:T(8,128)}, u32[]{:S(2)}) copy-start(f32[8,2,384,64]{2,3,1,0:T(8,128)} %fusion.55) | copy-start | bytes 4718596
  64.8 1.6 copy-start.2
  82.1 129.6 %all-to-all-start = ((bf16[8,64,2,384]{3,2,0,1:T(2,128)(2,1)}), bf16[8,64,2,384]{3,2,0,1:T(2,128)(2,1)S(1)}, u32[]{:S(2)}, u32[]{:S(2)}) async-start(bf16[8,64,2,384]{3,2,0,1:T(2,128)(2,1)} %copy.61), calls=%async_computation | async-start | bytes 1572864 | tf_op jit(solution)/shard_map/all_to_all | solution.py:81
  235.4 11.3 %copy-start.12 = (bf16[9,64,64]{2,1,0:T(8,128)(2,1)S(1)}, bf16[9,64,64]{2,1,0:T(8,128)(2,1)}, u32[]{:S(2)}) copy-start(bf16[9,64,64]{2,1,0:T(8,128)(2,1)} %param.5) | copy-start | bytes 221188
  235.6 11.4 %collective-permute-start.2 = (bf16[8,64,1,384]{3,1,2,0:T(8,128)(2,1)S(1)}, bf16[8,64,1,384]{3,1,2,0:T(8,128)(2,1)S(1)}, u32[]{:S(2)}, u32[]{:S(2)}) collective-permute-start(bf16[8,64,1,384]{3,1,2,0:T(8,128)(2,1)S(1)} %get-tuple-element.5), channel_id=1, source_target_pairs={{0,8},{8,16},{16,24},{24,32},{32,40},{40,48},{48,56},{56,64},{64,7... | collective-permute-start | bytes 1179656 | tf_op jit(solution)/shard_map/ppermute | solution.py:19
  241.4 9.1 %collective-permute-start.3 = (bf16[8,64,1,384]{3,1,2,0:T(8,128)(2,1)S(1)}, bf16[8,64,1,384]{3,1,2,0:T(8,128)(2,1)S(1)}, u32[]{:S(2)}, u32[]{:S(2)}) collective-permute-start(bf16[8,64,1,384]{3,1,2,0:T(8,128)(2,1)S(1)} %get-tuple-element.6), channel_id=1, source_target_pairs={{8,0},{16,8},{24,16},{32,24},{40,32},{48,40},{56,48},{64,56},{72,6... | collective-permute-start | bytes 1179656 | tf_op jit(solution)/shard_map/ppermute | solution.py:21
  254.0 1.1 copy-start.1
where the time goes:
time: 259 us; the launch traced here: 258 us
  blocking collectives  146 us (56%)
  matrix products  42.8 us (17%)
  starting transfers between devices  34.5 us (13%)
  waiting for transfers between devices  20.3 us (8%)
  local copies, waits for them, and re-layouts  10.6 us (4%)
  other arithmetic  2.89 us (1%)
    psum x1, blocking collectives, local(): scores = lax.psum(partial_scores * score_scale, 'space')  124 us
    dot_general x36, matrix products, convolve(): jnp.einsum('oc,mcyx->moyx', weights[3 * lat_shift + lon_shift], shifted,...  40.6 us
    all_to_all x1, blocking collectives, local(): lax.all_to_all(blended, 'mem', split_axis=0, concat_axis=1, tiled=True)  22.3 us
    all_to_all x1, waiting for transfers between devices, local(): lax.all_to_all(key_maps, 'mem', split_axis=1, concat_axis=0, tiled=True)  11.8 us
    ppermute x2, starting transfers between devices, with_halo(): lax.ppermute(tail, axis, [(i, (i + 1) % count) for i in range(ends)])  10.4 us
    all_to_all x1, starting transfers between devices, local(): lax.all_to_all(queries, 'mem', split_axis=1, concat_axis=0, tiled=True)  8.22 us
    ppermute x2, starting transfers between devices, with_halo(): lax.ppermute(head, axis, [((i + 1) % count, i) for i in range(ends)])  7.18 us
    ppermute x2, waiting for transfers between devices, with_halo(): lax.ppermute(head, axis, [((i + 1) % count, i) for i in range(ends)])  7.02 us
  transfers between devices with their start and end apart: 7, of which 4 were waited for; matrix products, arithmetic and copies ran while one was open for 12% of the time, Pallas kernels for 0%

commit v1 on v0

v1 whole, which is shorter than its diff:
```python
import math

import jax
import jax.numpy as jnp
from jax import lax
from jax.experimental import pallas as pl
from jax.experimental.pallas import tpu as pltpu
from jax.sharding import Mesh
from jax.sharding import PartitionSpec as P

C = 64
HEADS = 8
HD = 8
M = 64
ROWS = 2
LANES = ROWS * C
GROUPS = 8
LON = 384
LB = LON // GROUPS
LW = LB + 4
LV = LB + 2
SPACE = ("x", "y", "core")
BF = jnp.bfloat16
F32 = jnp.float32
VMEM_LIMIT = 48 * 1024 * 1024


def place_weights_kernel(w_ref, wo_ref, qk_ref, v_ref, o_ref):
    qk_ref[...] = jnp.zeros(qk_ref.shape, BF)
    v_ref[...] = jnp.zeros(v_ref.shape, BF)
    o_ref[...] = jnp.zeros(o_ref.shape, BF)
    for b in range(3):
        for a in range(3):
            tap = w_ref[3 * a + b]
            for ro in range(2):
                rin = 2 + ro + a - 1
                qk_ref[b, rin * C:(rin + 1) * C, ro * C:(ro + 1) * C] = tap[:, 0:C]
                qk_ref[b, rin * C:(rin + 1) * C, LANES + ro * C:LANES + (ro + 1) * C] = tap[:, C:2 * C]
            for ro in range(4):
                rin = ro + a
                v_ref[b, rin * C:(rin + 1) * C, ro * C:(ro + 1) * C] = tap[:, 2 * C:3 * C]
            for ro in range(2):
                rin = ro + a
                o_ref[b, rin * C:(rin + 1) * C, ro * C:(ro + 1) * C] = wo_ref[3 * a + b]


def place_weights(w_qkv, w_out):
    return pl.pallas_call(
        place_weights_kernel,
        out_shape=(
            jax.ShapeDtypeStruct((3, 6 * C, 4 * C), BF),
            jax.ShapeDtypeStruct((3, 6 * C, 4 * C), BF),
            jax.ShapeDtypeStruct((3, 4 * C, 2 * C), BF),
        ),
        compiler_params=pltpu.CompilerParams(vmem_limit_bytes=VMEM_LIMIT),
        cost_estimate=pl.CostEstimate(flops=0, bytes_accessed=1500000, transcendentals=0),
    )(jnp.swapaxes(w_qkv, 1, 2), jnp.swapaxes(w_out, 1, 2))


def conv_block(prev_ref, own_ref, next_ref, w_ref, start, count):
    total = None
    for b in range(3):
        window = pl.ds(start + b, count)
        x = jnp.concatenate([prev_ref[window], own_ref[window], next_ref[window]], axis=-1)
        part = jnp.dot(x.reshape(count * M, 6 * C), w_ref[b], preferred_element_type=F32)
        total = part if total is None else total + part
    return total


def head_of_lane(lanes):
    lane = lax.broadcasted_iota(jnp.int32, (1, lanes), 1)
    return (lane % C) // HD


def scores_kernel(prev_ref, own_ref, next_ref, w_ref, s_ref, acc_ref):
    acc_ref[...] = jnp.zeros(acc_ref.shape, F32)
    head = head_of_lane(2 * LANES)
    masks = [(head == h).astype(BF) for h in range(HEADS)]
    step = 8

    def chunk(i, carry):
        qk = conv_block(prev_ref, own_ref, next_ref, w_ref, 1 + i * step, step).astype(BF)
        q = qk[:, :LANES].reshape(step, M, LANES)
        k = qk[:, LANES:].reshape(step, M, LANES)
        part = None
        for l in range(0, step, 2):
            q2 = jnp.concatenate([q[l], q[l + 1]], axis=-1)
            k2 = jnp.concatenate([k[l], k[l + 1]], axis=-1)
            qm = jnp.concatenate([q2 * mask for mask in masks], axis=0)
            s = lax.dot_general(qm, k2, (((1,), (1,)), ((), ())), preferred_element_type=F32)
            part = s if part is None else part + s
        acc_ref[...] += part
        return carry

    lax.fori_loop(0, LB // step, chunk, 0)
    for h in range(HEADS):
        lo = acc_ref[h * M:h * M + M // 2]
        hi = acc_ref[h * M + M // 2:(h + 1) * M]
        s_ref[h] = jnp.concatenate([lo, hi], axis=-1)


def partial_scores(prev, own, after, w_qk):
    return pl.pallas_call(
        scores_kernel,
        out_shape=jax.ShapeDtypeStruct((HEADS, M // 2, 2 * M), F32),
        scratch_shapes=[pltpu.VMEM((HEADS * M, M), F32)],
        compiler_params=pltpu.CompilerParams(vmem_limit_bytes=VMEM_LIMIT),
        cost_estimate=pl.CostEstimate(flops=4_000_000_000, bytes_accessed=3000000, transcendentals=0),
    )(prev, own, after, w_qk)


def values_kernel(prev_ref, own_ref, next_ref, w_ref, keep_ref, v_ref):
    step = 10

    def chunk(i, carry):
        v = conv_block(prev_ref, own_ref, next_ref, w_ref, i * step, step)
        v = v.reshape(step, M, 4 * C) * keep_ref[pl.ds(i * step, step)]
        v_ref[pl.ds(i * step, step)] = v.astype(BF)
        return carry

    lax.fori_loop(0, LV // step, chunk, 0)


def value_maps(prev, own, after, w_v, keep):
    return pl.pallas_call(
        values_kernel,
        out_shape=jax.ShapeDtypeStruct((LV, M, 4 * C), BF),
        compiler_params=pltpu.CompilerParams(vmem_limit_bytes=VMEM_LIMIT),
        cost_estimate=pl.CostEstimate(flops=2_000_000_000, bytes_accessed=4000000, transcendentals=0),
    )(prev, own, after, w_v, keep)


def mix_kernel(attn_ref, v_ref, own_ref, w_ref, out_ref, att_ref):
    head = head_of_lane(4 * C)
    masks = [(head == h).astype(BF) for h in range(HEADS)]
    attn = jnp.concatenate(
        [jnp.concatenate([attn_ref[h][:, :M], attn_ref[h][:, M:]], axis=0) for h in range(HEADS)], axis=-1
    )

    def blend(t, carry):
        v = v_ref[t]
        vm = jnp.concatenate([v * mask for mask in masks], axis=0)
        att_ref[t] = jnp.dot(attn, vm, preferred_element_type=F32).astype(BF)
        return carry

    lax.fori_loop(0, LV, blend, 0, unroll=5)
    step = 8

    def chunk(i, carry):
        total = own_ref[pl.ds(i * step + 2, step)].astype(F32).reshape(step * M, LANES)
        for b in range(3):
            x = att_ref[pl.ds(i * step + b, step)].reshape(step * M, 4 * C)
            total = total + jnp.dot(x, w_ref[b], preferred_element_type=F32)
        out_ref[pl.ds(i * step, step)] = total.astype(BF).reshape(step, M, LANES)
        return carry

    lax.fori_loop(0, LB // step, chunk, 0)


def mix(attn, v, own, w_o):
    return pl.pallas_call(
        mix_kernel,
        out_shape=jax.ShapeDtypeStruct((LB, M, LANES), BF),
        scratch_shapes=[pltpu.VMEM((LV, M, 4 * C), BF)],
        compiler_params=pltpu.CompilerParams(vmem_limit_bytes=VMEM_LIMIT),
        cost_estimate=pl.CostEstimate(flops=4_000_000_000, bytes_accessed=4000000, transcendentals=0),
    )(attn, v, own, w_o)


def local(fields, w_qkv, w_out):
    members_here = fields.shape[0]
    place = lax.axis_index(SPACE)
    group = lax.axis_index("mem")
    last_place = lax.axis_size(SPACE) - 1
    w_qk, w_v, w_o = place_weights(w_qkv, w_out)

    cells = jnp.transpose(fields, (3, 0, 2, 1)).reshape(LON, members_here, LANES)
    padded = jnp.pad(cells, ((2, 2), (0, 0), (0, 0)))
    windows = jnp.stack([padded[g * LB:g * LB + LW] for g in range(GROUPS)])
    arrived = lax.all_to_all(windows, "mem", split_axis=0, concat_axis=0, tiled=True)
    own = jnp.transpose(arrived, (1, 0, 2, 3)).reshape(LW, M, LANES)
    prev = lax.ppermute(own, SPACE, [(i, i + 1) for i in range(last_place)])
    after = lax.ppermute(own, SPACE, [(i + 1, i) for i in range(last_place)])

    part = partial_scores(prev, own, after, w_qk)
    places = last_place + 1
    part = part.reshape(places, HEADS * M // 2 // places, 2 * M)
    part = lax.all_to_all(part, SPACE, split_axis=0, concat_axis=0, tiled=True).sum(axis=0)
    part = jnp.broadcast_to(part[None], (GROUPS,) + part.shape)
    part = lax.all_to_all(part, "mem", split_axis=0, concat_axis=0, tiled=True)
    row = lax.broadcasted_iota(jnp.int32, (LV, 1, 4 * C), 2) // C
    lon = lax.broadcasted_iota(jnp.int32, (LV, 1, 4 * C), 0)
    outside = (
        ((row == 0) & (place == 0))
        | ((row == 3) & (place == last_place))
        | ((lon == 0) & (group == 0))
        | ((lon == LV - 1) & (group == GROUPS - 1))
    )
    keep = jnp.where(outside, 0.0, 1.0).astype(F32)
    v = value_maps(prev, own, after, w_v, keep)
    part, v = lax.optimization_barrier((part, v))
    total = part.sum(axis=0)
    scale = 1.0 / math.sqrt(HD * ROWS * places * LON)
    attn = jax.nn.softmax((total * scale).reshape(-1, 2, M), axis=-1).astype(BF).reshape(total.shape)
    attn = jnp.broadcast_to(attn[None], (places,) + attn.shape)
    attn = lax.all_to_all(attn, SPACE, split_axis=0, concat_axis=0, tiled=True).reshape(HEADS, M // 2, 2 * M)
    mixed = mix(attn, v, own, w_o)
    mixed = jnp.transpose(mixed.reshape(LB, GROUPS, members_here, LANES), (1, 0, 2, 3))
    back = lax.all_to_all(mixed, "mem", split_axis=0, concat_axis=0, tiled=True)
    back = back.reshape(LON, members_here, ROWS, C)
    return jnp.transpose(back, (1, 3, 2, 0))


def solution(mesh):
    whole = Mesh(mesh.devices.reshape(4, 4, 2, 8), ("x", "y", "core", "mem"))
    return jax.shard_map(
        local,
        mesh=whole,
        in_specs=(P("mem", None, SPACE, None), P(), P()),
        out_specs=P("mem", None, SPACE, None),
        check_vma=False,
    )
```

time: 259 us -> 142 us (0.55)
  blocking collectives: 146 us -> 70.6 us
  matrix products: 42.8 us -> 0 us
  Pallas kernels: 0 us -> 18.9 us
  starting transfers between devices: 34.5 us -> 19.2 us
    psum x1 -> x0, blocking collectives: 124 us -> none  [local(): scores = lax.psum(partial_scores * score_scale, 'space')]
    all_to_all x1 -> x3, blocking collectives: 22.3 us -> 70.6 us  [the longest x1 32 us: local(): lax.all_to_all(windows, 'mem', split_axis=0, concat_axis=0, tiled=True)]
    dot_general x38 -> x0, matrix products: 42.8 us -> none  [the longest x36 40.6 us: convolve(): jnp.einsum('oc,mcyx->moyx', weights[3 * lat_shift + lon_shift], shifted,...]
    pallas_call x0 -> x4, Pallas kernels: none -> 18.9 us  [the longest x1 9.21 us: partial_scores(): pl.pallas_call(scores_kernel, out_shape=jax.ShapeDtypeStruct((HEADS, M //...]
    ppermute x4 -> x2, starting transfers between devices: 17.5 us -> 7.43 us  [the longest x1 5.51 us: local(): prev = lax.ppermute(own, SPACE, [(i, i + 1) for i in range(last_place)])]
    convert_element_type x4 -> x0, local copies, waits for them, and re-layouts: 6.83 us -> none  [the longest x3 5.14 us: project(): return convolve(padded_field, w_qkv[:, which_map * channels:(which_map +...]
    all_to_all x3 -> x2, starting transfers between devices: 16.9 us -> 11.7 us  [the longest x1 8.41 us: local(): lax.all_to_all(part, SPACE, split_axis=0, concat_axis=0, tiled=True)]
    all_to_all x3 -> x2, waiting for transfers between devices: 13.3 us -> 8.74 us  [the longest x1 7.52 us: local(): lax.all_to_all(part, SPACE, split_axis=0, concat_axis=0, tiled=True)]
  transfers between devices with their start and end apart: 7 -> 4, of which waited for: 4 -> 4; matrix products, arithmetic and copies ran while one was open for 12% -> 0% of each run, Pallas kernels for 0% -> 3%
where the time goes in v1:
time: 142 us
  blocking collectives  70.6 us (50%)
  waiting for transfers between devices  20.2 us (14%)
  starting transfers between devices  19.2 us (14%)
  Pallas kernels  18.9 us (13%)
  local copies, waits for them, and re-layouts  12.3 us (9%)
    all_to_all x1, blocking collectives, local(): lax.all_to_all(windows, 'mem', split_axis=0, concat_axis=0, tiled=True)  32 us
    all_to_all x1, blocking collectives, local(): back = lax.all_to_all(mixed, 'mem', split_axis=0, concat_axis=0, tiled=True)  26.5 us
    all_to_all x1, blocking collectives, local(): lax.all_to_all(attn, SPACE, split_axis=0, concat_axis=0, tiled=True)  12.1 us
    pallas_call x1, Pallas kernels, partial_scores(): pl.pallas_call(scores_kernel, out_shape=jax.ShapeDtypeStruct((HEADS, M //...  9.21 us
    all_to_all x1, starting transfers between devices, local(): lax.all_to_all(part, SPACE, split_axis=0, concat_axis=0, tiled=True)  8.41 us
    all_to_all x1, waiting for transfers between devices, local(): lax.all_to_all(part, SPACE, split_axis=0, concat_axis=0, tiled=True)  7.52 us
    ppermute x1, waiting for transfers between devices, local(): prev = lax.ppermute(own, SPACE, [(i, i + 1) for i in range(last_place)])  7.08 us
    pallas_call x1, Pallas kernels, mix(): pl.pallas_call(mix_kernel, out_shape=jax.ShapeDtypeStruct((LB, M, LANES),...  5.97 us
  transfers between devices with their start and end apart: 4, of which 4 were waited for; matrix products, arithmetic and copies ran while one was open for 0% of the time, Pallas kernels for 3%

profile of v1, /device:TPU:1, one launch (start us, length us, event | category | flops | bytes accessed | tf_op | source)
XLA Modules:
  0.0 141.9 jit_solution(3816128882690850724)
XLA Ops:
  0.0 1.3 copy.46
  1.3 0.2 fusion.2
  1.5 0.2 copy.30
  1.7 0.6 fusion.6
  2.4 0.2 copy.37
  2.6 0.2 copy.38
  2.8 0.2 copy.39
  3.0 0.2 copy.40
  3.1 0.2 copy.41
  3.3 0.2 copy.31
  3.7 32.0 %all_to_all.25 = bf16[8,52,8,128]{3,2,1,0:T(8,128)(2,1)S(1)} all-to-all(bf16[8,52,8,128]{3,2,1,0:T(8,128)(2,1)S(1)} %constant_dynamic-update-slice_fusion), channel_id=1, replica_groups=mesh['x'=4,'y'=4,'core'=2,'mem'=8] {'mem'}, dimensions={0} | all-to-all | bytes 1703936 | tf_op jit(solution)/shard_map/all_to_all | solution.py:180
  35.7 0.2 copy_bitcast_fusion.own_ref
  35.9 5.5 %collective-permute-start = (bf16[52,64,128]{2,1,0:T(8,128)(2,1)S(1)}, bf16[52,64,128]{2,1,0:T(8,128)(2,1)S(1)}, u32[]{:S(2)}, u32[]{:S(2)}) collective-permute-start(bf16[52,64,128]{2,1,0:T(8,128)(2,1)S(1)} %copy_bitcast_fusion.own_ref), channel_id=1, source_target_pairs={{0,8},{8,16},{16,24},{24,32},{32,40},{40,48},{48,56},{56,64},{64,7... | collective-permute-start | bytes 2555912 | tf_op jit(solution)/shard_map/ppermute | solution.py:182
  41.5 1.9 %collective-permute-start.1 = (bf16[52,64,128]{2,1,0:T(8,128)(2,1)S(1)}, bf16[52,64,128]{2,1,0:T(8,128)(2,1)S(1)}, u32[]{:S(2)}, u32[]{:S(2)}) collective-permute-start(bf16[52,64,128]{2,1,0:T(8,128)(2,1)S(1)} %copy_bitcast_fusion.own_ref), channel_id=1, source_target_pairs={{8,0},{16,8},{24,16},{32,24},{40,32},{48,40},{56,48},{64,56},{72,6... | collective-permute-start | bytes 2555912 | tf_op jit(solution)/shard_map/ppermute | solution.py:183
  43.6 0.4 shard_map.37
  44.0 7.1 %collective-permute-done.prev_ref = bf16[52,64,128]{2,1,0:T(8,128)(2,1)S(1)} collective-permute-done((bf16[52,64,128]{2,1,0:T(8,128)(2,1)S(1)}, bf16[52,64,128]{2,1,0:T(8,128)(2,1)S(1)}, u32[]{:S(2)}, u32[]{:S(2)}) %collective-permute-start) | collective-permute-done | bytes 852000 | tf_op jit(solution)/shard_map/ppermute | solution.py:182
  51.1 4.4 %collective-permute-done.1.next_ref = bf16[52,64,128]{2,1,0:T(8,128)(2,1)S(1)} collective-permute-done((bf16[52,64,128]{2,1,0:T(8,128)(2,1)S(1)}, bf16[52,64,128]{2,1,0:T(8,128)(2,1)S(1)}, u32[]{:S(2)}, u32[]{:S(2)}) %collective-permute-start.1) | collective-permute-done | bytes 852000 | tf_op jit(solution)/shard_map/ppermute | solution.py:183
  55.5 9.2 %shard_map.38 = f32[8,32,128]{2,1,0:T(8,128)} custom-call(bf16[52,64,128]{2,1,0:T(8,128)(2,1)S(1)} %collective-permute-done.prev_ref, bf16[52,64,128]{2,1,0:T(8,128)(2,1)S(1)} %copy_bitcast_fusion.own_ref, bf16[52,64,128]{2,1,0:T(8,128)(2,1)S(1)} %collective-permute-done.1.next_ref, bf16[3,384,256]{2,1,0:T(8,128)(2,1)S(1)} %get-tuple-element.10.w_ref), custom_call_target="tpu_custom_call" | custom-call | flops 4000000000 | bytes 3000000 | tf_op jit(solution)/shard_map/pallas_call | solution.py:103
  64.7 8.4 %all-to-all-start.1 = ((f32[32,8,128]{2,1,0:T(8,128)}), f32[32,8,128]{2,1,0:T(8,128)S(1)}, u32[]{:S(2)}, u32[]{:S(2)}) async-start(f32[32,8,128]{2,1,0:T(8,128)} %bitcast.14), calls=%async_computation.1 | async-start | bytes 262144 | tf_op jit(solution)/shard_map/all_to_all | solution.py:188
  73.3 7.5 %all-to-all-done.1 = f32[32,8,128]{2,1,0:T(8,128)S(1)} async-done(((f32[32,8,128]{2,1,0:T(8,128)}), f32[32,8,128]{2,1,0:T(8,128)S(1)}, u32[]{:S(2)}, u32[]{:S(2)}) %all-to-all-start.1) | async-done | bytes 131104 | tf_op jit(solution)/shard_map/all_to_all | solution.py:188
  80.8 0.6 broadcast_in_dim.12
  81.4 3.3 %all-to-all-start.2 = ((f32[8,8,128]{2,1,0:T(8,128)}), f32[8,8,128]{2,1,0:T(8,128)S(1)}, u32[]{:S(2)}, u32[]{:S(2)}) async-start(f32[8,8,128]{2,1,0:T(8,128)} %broadcast_in_dim.12), calls=%async_computation.2 | async-start | bytes 65536 | tf_op jit(solution)/shard_map/all_to_all | solution.py:190
  84.8 1.1 copy-done.2
  85.9 3.3 %shard_map.39.v_ref = bf16[50,64,256]{2,1,0:T(8,128)(2,1)S(1)} custom-call(bf16[52,64,128]{2,1,0:T(8,128)(2,1)S(1)} %collective-permute-done.prev_ref, bf16[52,64,128]{2,1,0:T(8,128)(2,1)S(1)} %copy_bitcast_fusion.own_ref, bf16[52,64,128]{2,1,0:T(8,128)(2,1)S(1)} %collective-permute-done.1.next_ref, bf16[3,384,256]{2,1,0:T(8,128)(2,1)S(1)} %copy-done.2, ...), custom_call_target="tpu_custom_call" | custom-call | flops 2000000000 | bytes 4000000 | tf_op jit(solution)/shard_map/pallas_call | solution.py:125
  89.2 1.2 copy-done.3
  90.4 1.2 all-to-all-done.2
  92.2 12.1 %all_to_all.26 = bf16[32,8,128]{2,1,0:T(8,128)(2,1)S(1)} all-to-all(bf16[32,8,128]{2,1,0:T(8,128)(2,1)S(1)} %broadcast_in_dim.24), channel_id=1, replica_groups=mesh['x'=4,'y'=4,'core'=2,'mem'=8] {'x','y','core'}, dimensions={0} | all-to-all | bytes 131072 | tf_op jit(solution)/shard_map/all_to_all | solution.py:206
  104.3 1.4 %copy-done.4 = bf16[50,64,256]{2,1,0:T(8,128)(2,1)S(1)} copy-done((bf16[50,64,256]{2,1,0:T(8,128)(2,1)S(1)}, bf16[50,64,256]{2,1,0:T(8,128)(2,1)}, u32[]{:S(2)}) %copy-start.4) | copy-done | bytes 1638424
  105.7 6.0 %shard_map.40 = bf16[48,64,128]{2,1,0:T(8,128)(2,1)S(1)} custom-call(bf16[8,32,128]{2,1,0:T(8,128)(2,1)S(1)} %bitcast.34, bf16[50,64,256]{2,1,0:T(8,128)(2,1)S(1)} %copy-done.4, bf16[52,64,128]{2,1,0:T(8,128)(2,1)S(1)} %copy_bitcast_fusion.own_ref, bf16[3,256,128]{2,1,0:T(8,128)(2,1)S(1)} %get-tuple-element.14.w_ref), custom_call_target="tpu_custom_call" | custom-call | flops 4000000000 | bytes 4000000 | tf_op jit(solution)/shard_map/pallas_call | solution.py:161
  111.8 26.5 %all_to_all.27 = bf16[8,48,8,128]{3,2,1,0:T(8,128)(2,1)S(1)} all-to-all(bf16[8,48,8,128]{3,2,1,0:T(8,128)(2,1)S(1)} %copy_bitcast_fusion.1), channel_id=1, replica_groups=mesh['x'=4,'y'=4,'core'=2,'mem'=8] {'mem'}, dimensions={0} | all-to-all | bytes 1572864 | tf_op jit(solution)/shard_map/all_to_all | solution.py:209
  138.3 0.7 reshape.184
  139.0 2.9 %copy.35 = bf16[8,64,2,384]{3,2,1,0:T(2,128)(2,1)} copy(bf16[8,64,2,384]{1,2,0,3:T(2,128)(2,1)S(1)} %bitcast.37) | data formatting | bytes 1572864 | tf_op jit(solution)/shard_map/transpose | solution.py:211
  (35 shorter events, 1.5 us)
Async XLA Ops:
  3.7 39.7 %copy-start.5 = (bf16[9,64,64]{2,1,0:T(8,128)(2,1)S(1)}, bf16[9,64,64]{2,1,0:T(8,128)(2,1)}, u32[]{:S(2)}) copy-start(bf16[9,64,64]{2,1,0:T(8,128)(2,1)} %param.5) | copy-start | bytes 221188
  3.7 39.9 %copy-start = (bf16[9,192,64]{1,2,0:T(8,128)(2,1)S(1)}, bf16[9,192,64]{1,2,0:T(8,128)(2,1)}, u32[]{:S(2)}) copy-start(bf16[9,192,64]{1,2,0:T(8,128)(2,1)} %param.4) | copy-start | bytes 663556
  35.9 15.1 %collective-permute-start = (bf16[52,64,128]{2,1,0:T(8,128)(2,1)S(1)}, bf16[52,64,128]{2,1,0:T(8,128)(2,1)S(1)}, u32[]{:S(2)}, u32[]{:S(2)}) collective-permute-start(bf16[52,64,128]{2,1,0:T(8,128)(2,1)S(1)} %copy_bitcast_fusion.own_ref), channel_id=1, source_target_pairs={{0,8},{8,16},{16,24},{24,32},{32,40},{40,48},{48,56},{56,64},{64,7... | collective-permute-start | bytes 2555912 | tf_op jit(solution)/shard_map/ppermute | solution.py:182
  41.5 14.0 %collective-permute-start.1 = (bf16[52,64,128]{2,1,0:T(8,128)(2,1)S(1)}, bf16[52,64,128]{2,1,0:T(8,128)(2,1)S(1)}, u32[]{:S(2)}, u32[]{:S(2)}) collective-permute-start(bf16[52,64,128]{2,1,0:T(8,128)(2,1)S(1)} %copy_bitcast_fusion.own_ref), channel_id=1, source_target_pairs={{8,0},{16,8},{24,16},{32,24},{40,32},{48,40},{56,48},{64,56},{72,6... | collective-permute-start | bytes 2555912 | tf_op jit(solution)/shard_map/ppermute | solution.py:183
  43.9 20.7 %copy-start.1 = (bf16[3,384,256]{2,1,0:T(8,128)(2,1)}, bf16[3,384,256]{2,1,0:T(8,128)(2,1)S(1)}, u32[]{:S(2)}) copy-start(bf16[3,384,256]{2,1,0:T(8,128)(2,1)S(1)} %get-tuple-element.11.w_ref) | copy-start | bytes 1769476
  64.7 16.1 %all-to-all-start.1 = ((f32[32,8,128]{2,1,0:T(8,128)}), f32[32,8,128]{2,1,0:T(8,128)S(1)}, u32[]{:S(2)}, u32[]{:S(2)}) async-start(f32[32,8,128]{2,1,0:T(8,128)} %bitcast.14), calls=%async_computation.1 | async-start | bytes 262144 | tf_op jit(solution)/shard_map/all_to_all | solution.py:188
  81.4 10.1 %all-to-all-start.2 = ((f32[8,8,128]{2,1,0:T(8,128)}), f32[8,8,128]{2,1,0:T(8,128)S(1)}, u32[]{:S(2)}, u32[]{:S(2)}) async-start(f32[8,8,128]{2,1,0:T(8,128)} %broadcast_in_dim.12), calls=%async_computation.2 | async-start | bytes 65536 | tf_op jit(solution)/shard_map/all_to_all | solution.py:190
  84.8 1.1 copy-start.2
  89.2 1.2 copy-start.3
  104.3 1.4 %copy-start.4 = (bf16[50,64,256]{2,1,0:T(8,128)(2,1)S(1)}, bf16[50,64,256]{2,1,0:T(8,128)(2,1)}, u32[]{:S(2)}) copy-start(bf16[50,64,256]{2,1,0:T(8,128)(2,1)} %copy-done.3) | copy-start | bytes 4915204

commit v2 on v1

v2 whole, which is shorter than its diff:
```python
import math

import jax
import jax.numpy as jnp
from jax import lax
from jax.experimental import pallas as pl
from jax.experimental.pallas import tpu as pltpu
from jax.sharding import Mesh
from jax.sharding import PartitionSpec as P

C = 64
HEADS = 8
HD = 8
M = 64
ROWS = 2
LANES = ROWS * C
GROUPS = 8
LON = 384
LB = LON // GROUPS
LW = LB + 4
LV = LB + 2
HALF = LB // 2
PACK = HALF + 4
SPACE = ("x", "y", "core")
BF = jnp.bfloat16
F32 = jnp.float32
VMEM_LIMIT = 24 * 1024 * 1024


def place_weights_kernel(core_ref, w_ref, wo_ref, qk_ref, near_ref, v_ref, o_ref):
    for ref in (qk_ref, near_ref, v_ref, o_ref):
        ref[...] = jnp.zeros(ref.shape, BF)

    def span(i):
        return slice(i * C, (i + 1) * C)

    def place(core):
        early, late = 1 - core, core
        near = -1 if core == 0 else 2
        far = -2 if core == 0 else 3
        mate = 2 if core == 0 else -2
        in_pair = {mate: 0, mate + 1: 1, 0: 2, 1: 3}
        in_all = {near: 0, far: 1, 0: 2, 1: 3, mate: 4, mate + 1: 5}
        for b in range(3):
            for a in range(3):
                tap = w_ref[3 * a + b]
                for out, part in ((early, 0), (late, 2)):
                    row = out + a - 1
                    if row in in_pair:
                        qk_ref[b, span(in_pair[row]), span(part)] = tap[:, 0:C]
                        qk_ref[b, span(in_pair[row]), span(part + 1)] = tap[:, C:2 * C]
                    else:
                        for half in range(2):
                            near_ref[span(2 * b + half), span(2 * half)] = tap[:, 0:C]
                            near_ref[span(2 * b + half), span(2 * half + 1)] = tap[:, C:2 * C]
                for out in range(-1, 3):
                    v_ref[b, span(in_all[out + a - 1]), span(out + 1)] = tap[:, 2 * C:3 * C]

    pl.when(core_ref[0] == 0)(lambda: place(0))
    pl.when(core_ref[0] == 1)(lambda: place(1))
    for b in range(3):
        for a in range(3):
            for out in range(2):
                o_ref[b, span(out + a), span(out)] = wo_ref[3 * a + b]


def params():
    return pltpu.CompilerParams(vmem_limit_bytes=VMEM_LIMIT)


def cost(flops, moved):
    return pl.CostEstimate(flops=flops, bytes_accessed=moved, transcendentals=0)


def place_weights(core, w_qkv, w_out):
    vmem = pl.BlockSpec(memory_space=pltpu.VMEM)
    return pl.pallas_call(
        place_weights_kernel,
        in_specs=[pl.BlockSpec(memory_space=pltpu.SMEM), vmem, vmem],
        out_shape=(
            jax.ShapeDtypeStruct((3, 4 * C, 4 * C), BF),
            jax.ShapeDtypeStruct((6 * C, 4 * C), BF),
            jax.ShapeDtypeStruct((3, 6 * C, 4 * C), BF),
            jax.ShapeDtypeStruct((3, 4 * C, 2 * C), BF),
        ),
        compiler_params=params(),
        cost_estimate=cost(0, 1500000),
    )(core.reshape(1), jnp.swapaxes(w_qkv, 1, 2), jnp.swapaxes(w_out, 1, 2))


def windows_kernel(rows_ref, out_ref, cells_ref):
    members = rows_ref.shape[0]
    edge = 2 * members
    cells_ref[:edge] = jnp.zeros((edge, LANES), F32)
    cells_ref[edge + LON * members:] = jnp.zeros((edge, LANES), F32)
    for m in range(members):
        cells_ref[pl.ds(edge + m, LON, stride=members)] = rows_ref[m].astype(F32).T
    for g in range(GROUPS):
        start = g * LB * members
        out_ref[g] = cells_ref[start:start + LW * members].astype(BF)


def windows_of(rows):
    members = rows.shape[0]
    return pl.pallas_call(
        windows_kernel,
        out_shape=jax.ShapeDtypeStruct((GROUPS, LW * members, LANES), BF),
        scratch_shapes=[pltpu.VMEM(((LON + 4) * members, LANES), F32)],
        compiler_params=params(),
        cost_estimate=cost(0, 1700000),
    )(rows)


def pack_kernel(row_ref, own_ref, packed_ref):
    for row in range(ROWS):
        lanes = slice(row * C, (row + 1) * C)

        @pl.when(row_ref[0] == row)
        def _():
            packed_ref[...] = jnp.concatenate([own_ref[:PACK, :, lanes], own_ref[LW - PACK:, :, lanes]], axis=-1)


def pack(row, own):
    return pl.pallas_call(
        pack_kernel,
        in_specs=[pl.BlockSpec(memory_space=pltpu.SMEM), pl.BlockSpec(memory_space=pltpu.VMEM)],
        out_shape=jax.ShapeDtypeStruct((PACK, M, LANES), BF),
        compiler_params=params(),
        cost_estimate=cost(0, 1300000),
    )(row.reshape(1), own)


def conv_rows(x, w_ref, count):
    total = None
    for b in range(3):
        part = jnp.dot(x[b:b + count].reshape(count * M, x.shape[-1]), w_ref[b], preferred_element_type=F32)
        total = part if total is None else total + part
    return total


def head_masks(lanes):
    lane = lax.broadcasted_iota(jnp.int32, (1, lanes), 1)
    head = (lane % C) // HD
    return [(head == h).astype(BF) for h in range(HEADS)]


def score_step(qk, count):
    masks = head_masks(LANES)
    q = jnp.concatenate([qk[l, :, :C] for l in range(count)], axis=-1)
    k = jnp.concatenate([qk[l, :, C:] for l in range(count)], axis=-1)
    pairs = [k[:, i * LANES:(i + 1) * LANES] for i in range(count // 2)]
    km = jnp.concatenate([jnp.concatenate([p * mask for p in pairs], axis=-1) for mask in masks], axis=0)
    return lax.dot_general(q, km, (((1,), (1,)), ((), ())), preferred_element_type=F32)


def early_kernel(mate_ref, own_ref, w_ref, s_ref, late_ref):
    step = 8
    total = None
    for i in range(LB // step):
        start = i * step
        window = slice(start + 1, start + step + 3)
        x = jnp.concatenate([mate_ref[window], own_ref[window]], axis=-1)
        qk = conv_rows(x, w_ref, step)
        late_ref[start:start + step] = qk[:, LANES:].reshape(step, M, LANES)
        part = score_step(qk[:, :LANES].astype(BF).reshape(step, M, LANES), step)
        total = part if total is None else total + part
    s_ref[...] = total


def late_kernel(near_ref, late_ref, first_ref, w_ref, s_ref):
    step = 12
    total = first_ref[...]
    for i in range(HALF // step):
        start = i * step
        x = jnp.concatenate([near_ref[start + 1 + b:start + 1 + b + step] for b in range(3)], axis=-1)
        add = jnp.dot(x.reshape(step * M, 6 * C), w_ref[...], preferred_element_type=F32)
        halves = []
        for half in range(2):
            at = half * HALF + start
            qk = late_ref[at:at + step].reshape(step * M, LANES) + add[:, half * LANES:(half + 1) * LANES]
            halves.append(qk.astype(BF).reshape(step, M, LANES))
        total = total + score_step(jnp.concatenate(halves, axis=0), 2 * step)
    for a in range(M // 8):
        for b in range(HEADS * M // 128):
            s_ref[a * (HEADS * M // 128) + b] = total[8 * a:8 * (a + 1), 128 * b:128 * (b + 1)]


def early_scores(mate, own, w_qk):
    return pl.pallas_call(
        early_kernel,
        out_shape=(jax.ShapeDtypeStruct((M, HEADS * M), F32), jax.ShapeDtypeStruct((LB, M, LANES), F32)),
        compiler_params=params(),
        cost_estimate=cost(3_000_000_000, 3000000),
    )(mate, own, w_qk)


def late_scores(near, late, first, w_near):
    tiles = HEADS * M * M // 1024
    return pl.pallas_call(
        late_kernel,
        out_shape=jax.ShapeDtypeStruct((tiles, 8, 128), F32),
        compiler_params=params(),
        cost_estimate=cost(2_000_000_000, 3000000),
    )(near, late, first, w_near)


def values_kernel(near_ref, far_ref, own_ref, mate_ref, w_ref, keep_ref, v_out, x_ref, v_ref, sems):
    half = LW // 2
    skip = half - (LW - PACK)
    x_ref[:half, :, :LANES] = jnp.concatenate([near_ref[:half, :, :C], far_ref[:half, :, :C]], axis=-1)
    x_ref[half:, :, :LANES] = jnp.concatenate([near_ref[skip:, :, C:], far_ref[skip:, :, C:]], axis=-1)
    step = 10
    w = w_ref[...].reshape(18 * C, 4 * C)
    copies = []
    for start in range(0, LV, step):
        x = jnp.concatenate(
            [ref[start + b:start + b + step] for b in range(3) for ref in (x_ref, own_ref, mate_ref)], axis=-1
        )
        v = jnp.dot(x.reshape(step * M, 18 * C), w, preferred_element_type=F32)
        piece = slice(start, start + step)
        v_ref[piece] = (v.reshape(step, M, 4 * C) * keep_ref[piece]).astype(BF)
        copies.append(pltpu.make_async_copy(v_ref.at[piece], v_out.at[piece], sems.at[start // step]))
        copies[-1].start()
    for copy in copies:
        copy.wait()


def value_maps(near, far, own, mate, w_v, keep):
    return pl.pallas_call(
        values_kernel,
        out_shape=pltpu.HBM((LV, M, 4 * C), BF),
        out_specs=pl.BlockSpec(memory_space=pltpu.HBM),
        scratch_shapes=[
            pltpu.VMEM((LW, M, LANES), BF),
            pltpu.VMEM((LV, M, 4 * C), BF),
            pltpu.SemaphoreType.DMA((5,)),
        ],
        compiler_params=params(),
        cost_estimate=cost(2_000_000_000, 4000000),
    )(near, far, own, mate, w_v, keep)


def mix_kernel(attn_ref, v_in, own_ref, w_ref, out_ref, v_ref, att_ref, sems):
    pieces = 5
    size = LV // pieces
    copies = [
        pltpu.make_async_copy(v_in.at[i * size:(i + 1) * size], v_ref.at[i * size:(i + 1) * size], sems.at[i])
        for i in range(pieces)
    ]
    for copy in copies:
        copy.start()
    masks = head_masks(4 * C)
    lane_tiles = HEADS * M // 128
    attn = jnp.concatenate(
        [jnp.concatenate([attn_ref[a * lane_tiles + b] for b in range(lane_tiles)], axis=-1) for a in range(M // 8)],
        axis=0,
    )
    for i in range(pieces):
        copies[i].wait()
        for t in range(i * size, (i + 1) * size):
            v = v_ref[t]
            vm = jnp.concatenate([v * mask for mask in masks], axis=0)
            att_ref[t] = jnp.dot(attn, vm, preferred_element_type=F32).astype(BF)
    step = 8
    for start in range(0, LB, step):
        total = own_ref[start + 2:start + 2 + step].astype(F32).reshape(step * M, LANES)
        for b in range(3):
            x = att_ref[start + b:start + b + step].reshape(step * M, 4 * C)
            total = total + jnp.dot(x, w_ref[b], preferred_element_type=F32)
        out_ref[start:start + step] = total.astype(BF).reshape(step, M, LANES)


def mix(attn, v, own, w_o):
    vmem = pl.BlockSpec(memory_space=pltpu.VMEM)
    hbm = pl.BlockSpec(memory_space=pltpu.HBM)
    return pl.pallas_call(
        mix_kernel,
        in_specs=[vmem, hbm, vmem, vmem],
        out_shape=jax.ShapeDtypeStruct((LB, M, LANES), BF),
        scratch_shapes=[
            pltpu.VMEM((LV, M, 4 * C), BF),
            pltpu.VMEM((LV, M, 4 * C), BF),
            pltpu.SemaphoreType.DMA((5,)),
        ],
        compiler_params=params(),
        cost_estimate=cost(4_000_000_000, 4000000),
    )(attn, pltpu.with_memory_space_constraint(v, pltpu.HBM), own, w_o)


def local(fields, w_qkv, w_out):
    members_here = fields.shape[0]
    core = lax.axis_index("core")
    place = lax.axis_index(SPACE)
    group = lax.axis_index("mem")
    places = lax.axis_size(SPACE)
    last_place = places - 1
    w_qk, w_near, w_v, w_o = place_weights(core, w_qkv, w_out)

    rows = jnp.transpose(fields, (0, 2, 1, 3)).reshape(members_here, LANES, LON)
    windows = windows_of(rows).reshape(GROUPS, LW, members_here, LANES)
    arrived = lax.all_to_all(windows, "mem", split_axis=0, concat_axis=0, tiled=True)
    own = jnp.transpose(arrived, (1, 0, 2, 3)).reshape(LW, M, LANES)
    seams = [(i, i + 1) for i in range(1, last_place, 2)]
    seams = seams + [(j, i) for i, j in seams]
    mate = lax.ppermute(own, "core", [(0, 1), (1, 0)])
    near = lax.ppermute(pack(core, own), SPACE, seams)
    far = lax.ppermute(pack(1 - core, own), SPACE, seams)

    first, late = early_scores(mate, own, w_qk)
    part = late_scores(near, late, first, w_near)
    part = lax.all_to_all(part, SPACE, split_axis=0, concat_axis=0, tiled=True)
    part = part.reshape((places, -1) + part.shape[1:]).sum(axis=0)
    part = jnp.broadcast_to(part[None], (GROUPS,) + part.shape)
    part = lax.all_to_all(part, "mem", split_axis=0, concat_axis=0, tiled=True)

    row = lax.broadcasted_iota(jnp.int32, (LV, 1, 4 * C), 2) // C
    lon = lax.broadcasted_iota(jnp.int32, (LV, 1, 4 * C), 0)
    outside = (
        ((row == 0) & (place == 0))
        | ((row == 3) & (place == last_place))
        | ((lon == 0) & (group == 0))
        | ((lon == LV - 1) & (group == GROUPS - 1))
    )
    keep = jnp.where(outside, 0.0, 1.0).astype(F32)
    v = value_maps(near, far, own, mate, w_v, keep)
    part, v = lax.optimization_barrier((part, v))
    total = part.sum(axis=0)
    scale = 1.0 / math.sqrt(HD * ROWS * places * LON)
    attn = jax.nn.softmax((total * scale).reshape(total.shape[:-1] + (2, M)), axis=-1).astype(BF).reshape(total.shape)
    attn = jnp.broadcast_to(attn[None], (places,) + attn.shape).reshape(-1, 8, 128)
    attn = lax.all_to_all(attn, SPACE, split_axis=0, concat_axis=0, tiled=True)
    mixed = mix(attn, v, own, w_o)
    mixed = jnp.transpose(mixed.reshape(LB, GROUPS, members_here, LANES), (1, 0, 2, 3))
    back = lax.all_to_all(mixed, "mem", split_axis=0, concat_axis=0, tiled=True)
    back = jnp.transpose(back.reshape(LON, members_here, LANES), (1, 2, 0))
    back = lax.optimization_barrier(back).reshape(members_here, ROWS, C, LON)
    return jnp.transpose(back, (0, 2, 1, 3))


def solution(mesh):
    whole = Mesh(mesh.devices.reshape(4, 4, 2, 8), ("x", "y", "core", "mem"))
    return jax.shard_map(
        local,
        mesh=whole,
        in_specs=(P("mem", None, SPACE, None), P(), P()),
        out_specs=P("mem", None, SPACE, None),
        check_vma=False,
    )
```

time: 142 us -> 125 us (0.88)
  waiting for transfers between devices: 20.2 us -> 10.3 us
  local copies, waits for them, and re-layouts: 12.3 us -> 5.06 us
  Pallas kernels: 18.9 us -> 17.1 us
    ppermute x2 -> x3, waiting for transfers between devices: 11.5 us -> 0.28 us  [the longest x1 0.28 us: local(): near = lax.ppermute(pack(core, own), SPACE, seams)]
    unnamed x21 -> x5, local copies, waits for them, and re-layouts: 5.19 us -> 0.16 us
    pallas_call x4 -> x8, Pallas kernels: 18.9 us -> 17.1 us  [the longest x1 5.18 us: mix(): pl.pallas_call(mix_kernel, in_specs=[vmem, hbm, vmem, vmem], out_shape=ja...]
    another operation x10 -> x0, local copies, waits for them, and re-layouts: 1.66 us -> none  [local(): windows = jnp.stack([padded[g * LB:g * LB + LW] for g in range(GROUPS)])]
    ppermute x2 -> x3, starting transfers between devices: 7.43 us -> 8.07 us  [the longest x1 3.12 us: local(): near = lax.ppermute(pack(core, own), SPACE, seams)]
    transpose x1 -> x2, local copies, waits for them, and re-layouts: 2.88 us -> 2.95 us  [the longest x1 1.69 us: local(): return jnp.transpose(back, (0, 2, 1, 3))]
  transfers between devices with their start and end apart: 4 -> 5, of which waited for: 4 -> 3; matrix products, arithmetic and copies ran while one was open for 0% -> 2% of each run, Pallas kernels for 3% -> 9%
where the time goes in v2:
time: 125 us; the launch traced here: 124 us
  blocking collectives  69.3 us (55%)
  starting transfers between devices  20.6 us (16%)
  Pallas kernels  17.1 us (14%)
  waiting for transfers between devices  10.3 us (8%)
  local copies, waits for them, and re-layouts  5.06 us (4%)
  other arithmetic  1.42 us (1%)
    all_to_all x1, blocking collectives, local(): lax.all_to_all(windows, 'mem', split_axis=0, concat_axis=0, tiled=True)  32 us
    all_to_all x1, blocking collectives, local(): back = lax.all_to_all(mixed, 'mem', split_axis=0, concat_axis=0, tiled=True)  25.2 us
    all_to_all x1, blocking collectives, local(): attn = lax.all_to_all(attn, SPACE, split_axis=0, concat_axis=0, tiled=True)  12.1 us
    all_to_all x1, starting transfers between devices, local(): part = lax.all_to_all(part, SPACE, split_axis=0, concat_axis=0, tiled=True)  9.19 us
    all_to_all x1, waiting for transfers between devices, local(): part = lax.all_to_all(part, SPACE, split_axis=0, concat_axis=0, tiled=True)  7.57 us
    pallas_call x1, Pallas kernels, mix(): pl.pallas_call(mix_kernel, in_specs=[vmem, hbm, vmem, vmem], out_shape=ja...  5.18 us
    pallas_call x1, Pallas kernels, value_maps(): pl.pallas_call(values_kernel, out_shape=pltpu.HBM((LV, M, 4 * C), BF), ou...  4.31 us
    pallas_call x1, Pallas kernels, early_scores(): pl.pallas_call(early_kernel, out_shape=(jax.ShapeDtypeStruct((M, HEADS *...  3.7 us
  transfers between devices with their start and end apart: 5, of which 3 were waited for; matrix products, arithmetic and copies ran while one was open for 2% of the time, Pallas kernels for 9%

profile of v2, /device:TPU:1, one launch (start us, length us, event | category | flops | bytes accessed | tf_op | source)
XLA Modules:
  0.0 124.0 jit_solution(16849971600237540064)
XLA Ops:
  0.0 1.3 %copy.13 = bf16[8,2,64,384]{3,2,1,0:T(8,128)(2,1)S(1)} copy(bf16[8,2,64,384]{3,1,2,0:T(2,128)(2,1)} %bitcast.29) | data formatting | bytes 1572864 | tf_op jit(solution)/shard_map/transpose | solution.py:299
  1.3 0.5 shard_map.37
  1.8 32.0 %all_to_all.25 = bf16[8,52,8,128]{3,2,1,0:T(8,128)(2,1)S(1)} all-to-all(bf16[8,52,8,128]{3,2,1,0:T(8,128)(2,1)S(1)} %bitcast.23), channel_id=1, replica_groups=mesh['x'=4,'y'=4,'core'=2,'mem'=8] {'mem'}, dimensions={0} | all-to-all | bytes 1703936 | tf_op jit(solution)/shard_map/all_to_all | solution.py:301
  33.8 0.2 copy_bitcast_fusion.own_ref
  34.0 2.5 %collective-permute-start.1 = (bf16[52,64,128]{2,1,0:T(8,128)(2,1)S(1)}, bf16[52,64,128]{2,1,0:T(8,128)(2,1)S(1)}, u32[]{:S(2)}, u32[]{:S(2)}) collective-permute-start(bf16[52,64,128]{2,1,0:T(8,128)(2,1)S(1)} %copy_bitcast_fusion.own_ref), channel_id=1, source_target_pairs={{0,8},{8,0},{1,9},{9,1},{2,10},{10,2},{3,11},{11,3},{4,12},{12,4},... | collective-permute-start | bytes 2555912 | tf_op jit(solution)/shard_map/ppermute | solution.py:305
  36.5 0.1 copy.15
  36.7 0.5 shard_map.39
  37.2 0.2 shard_map.38
  37.4 3.1 %collective-permute-start = (bf16[28,64,128]{2,1,0:T(8,128)(2,1)S(1)}, bf16[28,64,128]{2,1,0:T(8,128)(2,1)S(1)}, u32[]{:S(2)}, u32[]{:S(2)}) collective-permute-start(bf16[28,64,128]{2,1,0:T(8,128)(2,1)S(1)} %shard_map.38), channel_id=1, source_target_pairs={{8,16},{24,32},{40,48},{56,64},{72,80},{88,96},{104,112},{120,128}... | collective-permute-start | bytes 1376264 | tf_op jit(solution)/shard_map/ppermute | solution.py:306
  40.5 0.2 shard_map.42
  40.7 2.4 %collective-permute-start.2 = (bf16[28,64,128]{2,1,0:T(8,128)(2,1)S(1)}, bf16[28,64,128]{2,1,0:T(8,128)(2,1)}, u32[]{:S(2)}, u32[]{:S(2)}) collective-permute-start(bf16[28,64,128]{2,1,0:T(8,128)(2,1)S(1)} %shard_map.42), channel_id=1, source_target_pairs={{8,16},{24,32},{40,48},{56,64},{72,80},{88,96},{104,112},{120,128}... | collective-permute-start | bytes 1376264 | tf_op jit(solution)/shard_map/ppermute | solution.py:307
  43.2 3.7 %shard_map.40 = (f32[64,512]{1,0:T(8,128)S(1)}, f32[48,64,128]{2,1,0:T(8,128)S(1)}) custom-call(bf16[52,64,128]{2,1,0:T(8,128)(2,1)S(1)} %collective-permute-done.1.mate_ref, bf16[52,64,128]{2,1,0:T(8,128)(2,1)S(1)} %copy_bitcast_fusion.own_ref, bf16[3,256,256]{2,1,0:T(8,128)(2,1)S(1)} %get-tuple-element.13.w_ref), custom_call_target="tpu_custom_call" | custom-call | flops 3000000000 | bytes 3000000 | tf_op jit(solution)/shard_map/pallas_call | solution.py:189
  46.9 0.3 collective-permute-done.near_ref
  47.2 2.6 %shard_map.41 = f32[32,8,128]{2,1,0:T(8,128)} custom-call(bf16[28,64,128]{2,1,0:T(8,128)(2,1)S(1)} %collective-permute-done.near_ref, f32[48,64,128]{2,1,0:T(8,128)S(1)} %get-tuple-element.14.late_ref, f32[64,512]{1,0:T(8,128)S(1)} %get-tuple-element.15.first_ref, bf16[384,256]{1,0:T(8,128)(2,1)S(1)} %get-tuple-element.16.w_ref), custom_call_target="tpu_custom_call" | custom-call | flops 2000000000 | bytes 3000000 | tf_op jit(solution)/shard_map/pallas_call | solution.py:199
  49.8 9.2 %all-to-all-start.1 = ((f32[32,8,128]{2,1,0:T(8,128)}), f32[32,8,128]{2,1,0:T(8,128)}, u32[]{:S(2)}, u32[]{:S(2)}) async-start(f32[32,8,128]{2,1,0:T(8,128)} %shard_map.41), calls=%async_computation.1 | async-start | bytes 262144 | tf_op jit(solution)/shard_map/all_to_all | solution.py:311
  59.0 0.2 or_select_fusion.keep_ref
  59.2 7.6 %all-to-all-done.1 = f32[32,8,128]{2,1,0:T(8,128)} async-done(((f32[32,8,128]{2,1,0:T(8,128)}), f32[32,8,128]{2,1,0:T(8,128)}, u32[]{:S(2)}, u32[]{:S(2)}) %all-to-all-start.1) | async-done | bytes 131104 | tf_op jit(solution)/shard_map/all_to_all | solution.py:311
  66.7 0.9 reduce_sum.27
  67.7 0.6 broadcast_in_dim.10
  68.3 3.3 %all-to-all-start.2 = ((f32[8,1,8,128]{3,2,1,0:T(8,128)}), f32[8,1,8,128]{3,2,1,0:T(8,128)S(1)}, u32[]{:S(2)}, u32[]{:S(2)}) async-start(f32[8,1,8,128]{3,2,1,0:T(8,128)} %broadcast_in_dim.10), calls=%async_computation.2 | async-start | bytes 65536 | tf_op jit(solution)/shard_map/all_to_all | solution.py:314
  71.7 4.3 %shard_map.43.v_in = bf16[50,64,256]{2,1,0:T(8,128)(2,1)} custom-call(bf16[28,64,128]{2,1,0:T(8,128)(2,1)S(1)} %collective-permute-done.near_ref, bf16[28,64,128]{2,1,0:T(8,128)(2,1)} %collective-permute-done.2.far_ref, bf16[52,64,128]{2,1,0:T(8,128)(2,1)S(1)} %copy_bitcast_fusion.own_ref, bf16[52,64,128]{2,1,0:T(8,128)(2,1)S(1)} %collective-permute-done.1.mate_ref, ...), custom_call_target="tpu_custom_call" | custom-call | flops 2000000000 | bytes 4000000 | tf_op jit(solution)/shard_map/pallas_call | solution.py:229
  76.0 2.5 %all-to-all-done.2 = f32[8,1,8,128]{3,2,1,0:T(8,128)S(1)} async-done(((f32[8,1,8,128]{3,2,1,0:T(8,128)}), f32[8,1,8,128]{3,2,1,0:T(8,128)S(1)}, u32[]{:S(2)}, u32[]{:S(2)}) %all-to-all-start.2) | async-done | bytes 32800 | tf_op jit(solution)/shard_map/all_to_all | solution.py:314
  78.5 0.1 reduce_max.9
  78.6 0.2 exponential_reduce_fusion
  78.9 0.1 div.30
  79.0 0.1 sub.42
  79.1 12.1 %all_to_all.26.attn_ref = bf16[32,8,128]{2,1,0:T(8,128)(2,1)S(1)} all-to-all(bf16[32,8,128]{2,1,0:T(8,128)(2,1)S(1)} %reshape.229), channel_id=1, replica_groups=mesh['x'=4,'y'=4,'core'=2,'mem'=8] {'x','y','core'}, dimensions={0} | all-to-all | bytes 131072 | tf_op jit(solution)/shard_map/all_to_all | solution.py:331
  91.2 5.2 %shard_map.44 = bf16[48,64,128]{2,1,0:T(8,128)(2,1)S(1)} custom-call(bf16[32,8,128]{2,1,0:T(8,128)(2,1)S(1)} %all_to_all.26.attn_ref, bf16[50,64,256]{2,1,0:T(8,128)(2,1)} %shard_map.43.v_in, bf16[52,64,128]{2,1,0:T(8,128)(2,1)S(1)} %copy_bitcast_fusion.own_ref, bf16[3,256,128]{2,1,0:T(8,128)(2,1)S(1)} %get-tuple-element.20.w_ref), custom_call_target="tpu_custom_call" | custom-call | flops 4000000000 | bytes 4000000 | tf_op jit(solution)/shard_map/pallas_call | solution.py:276
  96.4 0.1 copy_bitcast_fusion.1
  96.6 25.2 %all_to_all.27 = bf16[8,48,8,128]{3,2,1,0:T(8,128)(2,1)S(1)} all-to-all(bf16[8,48,8,128]{3,2,1,0:T(8,128)(2,1)S(1)} %copy_bitcast_fusion.1), channel_id=1, replica_groups=mesh['x'=4,'y'=4,'core'=2,'mem'=8] {'mem'}, dimensions={0} | all-to-all | bytes 1572864 | tf_op jit(solution)/shard_map/all_to_all | solution.py:334
  121.8 0.6 copy.17
  122.4 1.7 %copy.18 = bf16[8,64,2,384]{3,2,1,0:T(2,128)(2,1)} copy(bf16[8,64,2,384]{3,1,2,0:T(8,128)(2,1)S(1)} %bitcast.28) | data formatting | bytes 1572864 | tf_op jit(solution)/shard_map/transpose | solution.py:337
  (16 shorter events, 0.3 us)
Async XLA Ops:
  1.7 34.8 %copy-start.1 = (bf16[9,64,64]{2,1,0:T(8,128)(2,1)S(1)}, bf16[9,64,64]{2,1,0:T(8,128)(2,1)}, u32[]{:S(2)}) copy-start(bf16[9,64,64]{2,1,0:T(8,128)(2,1)} %param.5) | copy-start | bytes 221188
  1.8 34.9 %copy-start = (bf16[9,192,64]{1,2,0:T(8,128)(2,1)S(1)}, bf16[9,192,64]{1,2,0:T(8,128)(2,1)}, u32[]{:S(2)}) copy-start(bf16[9,192,64]{1,2,0:T(8,128)(2,1)} %param.4) | copy-start | bytes 663556
  34.0 9.2 %collective-permute-start.1 = (bf16[52,64,128]{2,1,0:T(8,128)(2,1)S(1)}, bf16[52,64,128]{2,1,0:T(8,128)(2,1)S(1)}, u32[]{:S(2)}, u32[]{:S(2)}) collective-permute-start(bf16[52,64,128]{2,1,0:T(8,128)(2,1)S(1)} %copy_bitcast_fusion.own_ref), channel_id=1, source_target_pairs={{0,8},{8,0},{1,9},{9,1},{2,10},{10,2},{3,11},{11,3},{4,12},{12,4},... | collective-permute-start | bytes 2555912 | tf_op jit(solution)/shard_map/ppermute | solution.py:305
  37.4 9.8 %collective-permute-start = (bf16[28,64,128]{2,1,0:T(8,128)(2,1)S(1)}, bf16[28,64,128]{2,1,0:T(8,128)(2,1)S(1)}, u32[]{:S(2)}, u32[]{:S(2)}) collective-permute-start(bf16[28,64,128]{2,1,0:T(8,128)(2,1)S(1)} %shard_map.38), channel_id=1, source_target_pairs={{8,16},{24,32},{40,48},{56,64},{72,80},{88,96},{104,112},{120,128}... | collective-permute-start | bytes 1376264 | tf_op jit(solution)/shard_map/ppermute | solution.py:306
  40.7 30.9 %collective-permute-start.2 = (bf16[28,64,128]{2,1,0:T(8,128)(2,1)S(1)}, bf16[28,64,128]{2,1,0:T(8,128)(2,1)}, u32[]{:S(2)}, u32[]{:S(2)}) collective-permute-start(bf16[28,64,128]{2,1,0:T(8,128)(2,1)S(1)} %shard_map.42), channel_id=1, source_target_pairs={{8,16},{24,32},{40,48},{56,64},{72,80},{88,96},{104,112},{120,128}... | collective-permute-start | bytes 1376264 | tf_op jit(solution)/shard_map/ppermute | solution.py:307
  49.8 16.9 %all-to-all-start.1 = ((f32[32,8,128]{2,1,0:T(8,128)}), f32[32,8,128]{2,1,0:T(8,128)}, u32[]{:S(2)}, u32[]{:S(2)}) async-start(f32[32,8,128]{2,1,0:T(8,128)} %shard_map.41), calls=%async_computation.1 | async-start | bytes 262144 | tf_op jit(solution)/shard_map/all_to_all | solution.py:311
  68.3 10.1 %all-to-all-start.2 = ((f32[8,1,8,128]{3,2,1,0:T(8,128)}), f32[8,1,8,128]{3,2,1,0:T(8,128)S(1)}, u32[]{:S(2)}, u32[]{:S(2)}) async-start(f32[8,1,8,128]{3,2,1,0:T(8,128)} %broadcast_in_dim.10), calls=%async_computation.2 | async-start | bytes 65536 | tf_op jit(solution)/shard_map/all_to_all | solution.py:314

commit v3 on v2

--- a/solution.py
+++ b/solution.py
@@ -1,3 +1,4 @@
+import functools
 import math
 
 import jax
@@ -27,9 +28,13 @@
 VMEM_LIMIT = 24 * 1024 * 1024
 
 
-def place_weights_kernel(core_ref, w_ref, wo_ref, qk_ref, near_ref, v_ref, o_ref):
-    for ref in (qk_ref, near_ref, v_ref, o_ref):
+def place_weights_kernel(core_ref, w_ref, wo_ref, qk_ref, near_ref, v_ref, o_ref, plain_ref):
+    for ref in (qk_ref, near_ref, plain_ref):
         ref[...] = jnp.zeros(ref.shape, BF)
+    new = lax.broadcasted_iota(jnp.int32, (4 * C, 4 * C), 0)
+    old = lax.broadcasted_iota(jnp.int32, (4 * C, 4 * C), 1)
+    wanted = new % (4 * HD) // HD * C + new // (4 * HD) * HD + new % HD
+    order = (wanted == old).astype(BF)
 
     def span(i):
         return slice(i * C, (i + 1) * C)
@@ -54,14 +59,20 @@
                             near_ref[span(2 * b + half), span(2 * half)] = tap[:, 0:C]
                             near_ref[span(2 * b + half), span(2 * half + 1)] = tap[:, C:2 * C]
                 for out in range(-1, 3):
-                    v_ref[b, span(in_all[out + a - 1]), span(out + 1)] = tap[:, 2 * C:3 * C]
+                    plain_ref[b, span(in_all[out + a - 1]), span(out + 1)] = tap[:, 2 * C:3 * C]
 
     pl.when(core_ref[0] == 0)(lambda: place(0))
     pl.when(core_ref[0] == 1)(lambda: place(1))
     for b in range(3):
+        v_ref[b] = lax.dot_general(
+            plain_ref[b], order, (((1,), (1,)), ((), ())), preferred_element_type=F32
+        ).astype(BF)
+    plain_ref[...] = jnp.zeros(plain_ref.shape, BF)
+    for b in range(3):
         for a in range(3):
             for out in range(2):
-                o_ref[b, span(out + a), span(out)] = wo_ref[3 * a + b]
+                plain_ref[b, span(out + a), span(out)] = wo_ref[3 * a + b]
+        o_ref[b] = jnp.dot(order, plain_ref[b, :4 * C, :2 * C], preferred_element_type=F32).astype(BF)
 
 
 def params():
@@ -83,6 +94,7 @@
             jax.ShapeDtypeStruct((3, 6 * C, 4 * C), BF),
             jax.ShapeDtypeStruct((3, 4 * C, 2 * C), BF),
         ),
+        scratch_shapes=[pltpu.VMEM((3, 6 * C, 4 * C), BF)],
         compiler_params=params(),
         cost_estimate=cost(0, 1500000),
     )(core.reshape(1), jnp.swapaxes(w_qkv, 1, 2), jnp.swapaxes(w_out, 1, 2))
@@ -249,7 +261,8 @@
     ]
     for copy in copies:
         copy.start()
-    masks = head_masks(4 * C)
+    lane = lax.broadcasted_iota(jnp.int32, (1, 4 * C), 1) % LANES
+    masks = [(lane // (4 * HD) == h).astype(BF) for h in range(HEADS // 2)]
     lane_tiles = HEADS * M // 128
     attn = jnp.concatenate(
         [jnp.concatenate([attn_ref[a * lane_tiles + b] for b in range(lane_tiles)], axis=-1) for a in range(M // 8)],
@@ -257,10 +270,15 @@
     )
     for i in range(pieces):
         copies[i].wait()
-        for t in range(i * size, (i + 1) * size):
-            v = v_ref[t]
-            vm = jnp.concatenate([v * mask for mask in masks], axis=0)
-            att_ref[t] = jnp.dot(attn, vm, preferred_element_type=F32).astype(BF)
+        for t in range(i * size, (i + 1) * size, 2):
+            for half in range(2):
+                lanes = slice(half * LANES, (half + 1) * LANES)
+                v = jnp.concatenate([v_ref[t, :, lanes], v_ref[t + 1, :, lanes]], axis=-1)
+                vm = jnp.concatenate([v * mask for mask in masks], axis=0)
+                weights = attn[:, half * 4 * M:(half + 1) * 4 * M]
+                blended = jnp.dot(weights, vm, preferred_element_type=F32).astype(BF)
+                att_ref[t, :, lanes] = blended[:, :LANES]
+                att_ref[t + 1, :, lanes] = blended[:, LANES:]
     step = 8
     for start in range(0, LB, step):
         total = own_ref[start + 2:start + 2 + step].astype(F32).reshape(step * M, LANES)
@@ -287,6 +305,72 @@
     )(attn, pltpu.with_memory_space_constraint(v, pltpu.HBM), own, w_o)
 
 
+def total_kernel(parts_ref, out_ref):
+    total = parts_ref[0]
+    for i in range(1, parts_ref.shape[0]):
+        total = total + parts_ref[i]
+    for g in range(out_ref.shape[0]):
+        out_ref[g] = total
+
+
+def summed(parts, copies):
+    return pl.pallas_call(
+        total_kernel,
+        out_shape=jax.ShapeDtypeStruct((copies,) + parts.shape[1:], F32),
+        compiler_params=params(),
+        cost_estimate=cost(0, 300000),
+    )(parts)
+
+
+def softmax_kernel(scale, parts_ref, out_ref):
+    total = parts_ref[0]
+    for i in range(1, parts_ref.shape[0]):
+        total = total + parts_ref[i]
+    total = total * scale
+    low = lax.broadcasted_iota(jnp.int32, total.shape, 1) < M
+
+    def halves(reduce, x, fill):
+        first = reduce(jnp.where(low, x, fill), axis=-1, keepdims=True)
+        second = reduce(jnp.where(low, fill, x), axis=-1, keepdims=True)
+        return jnp.where(low, first, second)
+
+    e = jnp.exp(total - halves(jnp.max, total, -jnp.inf))
+    attn = (e / halves(jnp.sum, e, 0.0)).astype(BF)
+    for g in range(out_ref.shape[0]):
+        out_ref[g] = attn
+
+
+def softmax_of(parts, scale, copies):
+    return pl.pallas_call(
+        functools.partial(softmax_kernel, scale),
+        out_shape=jax.ShapeDtypeStruct((copies,) + parts.shape[1:], BF),
+        compiler_params=params(),
+        cost_estimate=cost(0, 300000),
+    )(parts)
+
+
+def final_kernel(back_ref, out_ref, cells_ref):
+    members = out_ref.shape[0]
+    count = LB * members
+    for g in range(GROUPS):
+        cells_ref[g * count:(g + 1) * count] = back_ref[g].astype(F32)
+    for m in range(members):
+        rows = cells_ref[pl.ds(m, LON, stride=members)].T
+        for r in range(ROWS):
+            out_ref[m, :, r] = rows[r * C:(r + 1) * C].astype(BF)
+
+
+def final_layout(back):
+    members = back.shape[1] // LB
+    return pl.pallas_call(
+        final_kernel,
+        out_shape=jax.ShapeDtypeStruct((members, C, ROWS, LON), BF),
+        scratch_shapes=[pltpu.VMEM((LON * members, LANES), F32)],
+        compiler_params=params(),
+        cost_estimate=cost(0, 1600000),
+    )(back)
+
+
 def local(fields, w_qkv, w_out):
     members_here = fields.shape[0]
     core = lax.axis_index("core")
@@ -294,7 +378,6 @@
     group = lax.axis_index("mem")
     places = lax.axis_size(SPACE)
     last_place = places - 1
-    w_qk, w_near, w_v, w_o = place_weights(core, w_qkv, w_out)
 
     rows = jnp.transpose(fields, (0, 2, 1, 3)).reshape(members_here, LANES, LON)
     windows = windows_of(rows).reshape(GROUPS, LW, members_here, LANES)
@@ -302,18 +385,14 @@
     own = jnp.transpose(arrived, (1, 0, 2, 3)).reshape(LW, M, LANES)
     seams = [(i, i + 1) for i in range(1, last_place, 2)]
     seams = seams + [(j, i) for i, j in seams]
+    near = lax.ppermute(pack(core, own), SPACE, seams)
     mate = lax.ppermute(own, "core", [(0, 1), (1, 0)])
-    near = lax.ppermute(pack(core, own), SPACE, seams)
     far = lax.ppermute(pack(1 - core, own), SPACE, seams)
-
+    w_qk, w_near, w_v, w_o = place_weights(core, w_qkv, w_out)
     first, late = early_scores(mate, own, w_qk)
     part = late_scores(near, late, first, w_near)
-    part = lax.all_to_all(part, SPACE, split_axis=0, concat_axis=0, tiled=True)
-    part = part.reshape((places, -1) + part.shape[1:]).sum(axis=0)
-    part = jnp.broadcast_to(part[None], (GROUPS,) + part.shape)
-    part = lax.all_to_all(part, "mem", split_axis=0, concat_axis=0, tiled=True)
-
-    row = lax.broadcasted_iota(jnp.int32, (LV, 1, 4 * C), 2) // C
+
+    row = lax.broadcasted_iota(jnp.int32, (LV, 1, 4 * C), 2) % (4 * HD) // HD
     lon = lax.broadcasted_iota(jnp.int32, (LV, 1, 4 * C), 0)
     outside = (
         ((row == 0) & (place == 0))
@@ -322,19 +401,16 @@
         | ((lon == LV - 1) & (group == GROUPS - 1))
     )
     keep = jnp.where(outside, 0.0, 1.0).astype(F32)
+    part = lax.all_to_all(part, SPACE, split_axis=0, concat_axis=0, tiled=True)
     v = value_maps(near, far, own, mate, w_v, keep)
     part, v = lax.optimization_barrier((part, v))
-    total = part.sum(axis=0)
-    scale = 1.0 / math.sqrt(HD * ROWS * places * LON)
-    attn = jax.nn.softmax((total * scale).reshape(total.shape[:-1] + (2, M)), axis=-1).astype(BF).reshape(total.shape)
-    attn = jnp.broadcast_to(attn[None], (places,) + attn.shape).reshape(-1, 8, 128)
+    part = lax.all_to_all(summed(part, GROUPS), "mem", split_axis=0, concat_axis=0, tiled=True)
+    attn = softmax_of(part, 1.0 / math.sqrt(HD * ROWS * places * LON), places)
     attn = lax.all_to_all(attn, SPACE, split_axis=0, concat_axis=0, tiled=True)
     mixed = mix(attn, v, own, w_o)
     mixed = jnp.transpose(mixed.reshape(LB, GROUPS, members_here, LANES), (1, 0, 2, 3))
     back = lax.all_to_all(mixed, "mem", split_axis=0, concat_axis=0, tiled=True)
-    back = jnp.transpose(back.reshape(LON, members_here, LANES), (1, 2, 0))
-    back = lax.optimization_barrier(back).reshape(members_here, ROWS, C, LON)
-    return jnp.transpose(back, (0, 2, 1, 3))
+    return final_layout(back.reshape(GROUPS, LB * members_here, LANES))
 
 
 def solution(mesh):

time: 125 us -> 121 us (0.968)
  blocking collectives: 69.3 us -> 79.6 us
  waiting for transfers between devices: 10.3 us -> 3.4 us
  starting transfers between devices: 20.6 us -> 17.2 us
  local copies, waits for them, and re-layouts: 5.06 us -> 1.8 us
    all_to_all x0 -> x1, blocking collectives: none -> 9.24 us  [local(): lax.all_to_all(summed(part, GROUPS), 'mem', split_axis=0, concat_axis=0,...]
    all_to_all x1, waiting for transfers between devices: 7.57 us -> 3.29 us  [local(): part = lax.all_to_all(part, SPACE, split_axis=0, concat_axis=0, tiled=True)]
    all_to_all x1 -> x0, starting transfers between devices: 3.34 us -> none  [local(): part = lax.all_to_all(part, 'mem', split_axis=0, concat_axis=0, tiled=True)]
    all_to_all x1 -> x0, waiting for transfers between devices: 2.46 us -> none  [local(): part = lax.all_to_all(part, 'mem', split_axis=0, concat_axis=0, tiled=True)]
    pallas_call x0 -> x3, Pallas kernels: none -> 1.91 us  [the longest x1 1.71 us: final_layout(): pl.pallas_call(final_kernel, out_shape=jax.ShapeDtypeStruct((members, C,...]
    transpose x1 -> x0, local copies, waits for them, and re-layouts: 1.69 us -> none  [local(): return jnp.transpose(back, (0, 2, 1, 3))]
  transfers between devices with their start and end apart: 5 -> 4, of which waited for: 3 -> 2; matrix products, arithmetic and copies ran while one was open for 2% -> 0% of each run, Pallas kernels for 9% -> 10%
where the time goes in v3:
time: 121 us
  blocking collectives  79.6 us (66%)
  Pallas kernels  18.3 us (15%)
  starting transfers between devices  17.2 us (14%)
  waiting for transfers between devices  3.4 us (3%)
  local copies, waits for them, and re-layouts  1.8 us (1%)
    all_to_all x1, blocking collectives, local(): lax.all_to_all(windows, 'mem', split_axis=0, concat_axis=0, tiled=True)  32 us
    all_to_all x1, blocking collectives, local(): back = lax.all_to_all(mixed, 'mem', split_axis=0, concat_axis=0, tiled=True)  26 us
    all_to_all x1, blocking collectives, local(): attn = lax.all_to_all(attn, SPACE, split_axis=0, concat_axis=0, tiled=True)  12.4 us
    all_to_all x1, blocking collectives, local(): lax.all_to_all(summed(part, GROUPS), 'mem', split_axis=0, concat_axis=0,...  9.24 us
    all_to_all x1, starting transfers between devices, local(): part = lax.all_to_all(part, SPACE, split_axis=0, concat_axis=0, tiled=True)  9.13 us
    pallas_call x1, Pallas kernels, value_maps(): pl.pallas_call(values_kernel, out_shape=pltpu.HBM((LV, M, 4 * C), BF), ou...  4.38 us
    pallas_call x1, Pallas kernels, mix(): pl.pallas_call(mix_kernel, in_specs=[vmem, hbm, vmem, vmem], out_shape=ja...  4.06 us
    pallas_call x1, Pallas kernels, early_scores(): pl.pallas_call(early_kernel, out_shape=(jax.ShapeDtypeStruct((M, HEADS *...  3.7 us
  transfers between devices with their start and end apart: 4, of which 2 were waited for; matrix products, arithmetic and copies ran while one was open for 0% of the time, Pallas kernels for 10%

profile of v3, /device:TPU:1, one launch (start us, length us, event | category | flops | bytes accessed | tf_op | source)
XLA Modules:
  0.0 120.8 jit_solution(6261058451244840469)
XLA Ops:
  0.0 1.3 %copy.8 = bf16[8,2,64,384]{3,2,1,0:T(8,128)(2,1)S(1)} copy(bf16[8,2,64,384]{3,1,2,0:T(2,128)(2,1)} %bitcast.23) | data formatting | bytes 1572864 | tf_op jit(solution)/shard_map/transpose | solution.py:382
  1.3 0.5 shard_map.37
  1.7 0.0 copy-start.3
  1.8 0.0 copy-start
  1.8 32.0 %all_to_all.25 = bf16[8,52,8,128]{3,2,1,0:T(8,128)(2,1)S(1)} all-to-all(bf16[8,52,8,128]{3,2,1,0:T(8,128)(2,1)S(1)} %bitcast.18), channel_id=1, replica_groups=mesh['x'=4,'y'=4,'core'=2,'mem'=8] {'mem'}, dimensions={0} | all-to-all | bytes 1703936 | tf_op jit(solution)/shard_map/all_to_all | solution.py:384
  33.8 0.2 copy_bitcast_fusion.own_ref
  34.0 2.5 %collective-permute-start.1 = (bf16[52,64,128]{2,1,0:T(8,128)(2,1)S(1)}, bf16[52,64,128]{2,1,0:T(8,128)(2,1)S(1)}, u32[]{:S(2)}, u32[]{:S(2)}) collective-permute-start(bf16[52,64,128]{2,1,0:T(8,128)(2,1)S(1)} %copy_bitcast_fusion.own_ref), channel_id=1, source_target_pairs={{0,8},{8,0},{1,9},{9,1},{2,10},{10,2},{3,11},{11,3},{4,12},{12,4},... | collective-permute-start | bytes 2555912 | tf_op jit(solution)/shard_map/ppermute | solution.py:389
  36.5 0.1 copy.10
  36.7 0.0 copy-done
  36.7 0.8 shard_map.39
  37.5 0.0 copy-start.1
  37.5 0.2 shard_map.38
  37.7 3.1 %collective-permute-start = (bf16[28,64,128]{2,1,0:T(8,128)(2,1)S(1)}, bf16[28,64,128]{2,1,0:T(8,128)(2,1)S(1)}, u32[]{:S(2)}, u32[]{:S(2)}) collective-permute-start(bf16[28,64,128]{2,1,0:T(8,128)(2,1)S(1)} %shard_map.38), channel_id=1, source_target_pairs={{8,16},{24,32},{40,48},{56,64},{72,80},{88,96},{104,112},{120,128}... | collective-permute-start | bytes 1376264 | tf_op jit(solution)/shard_map/ppermute | solution.py:388
  40.9 0.2 or_select_fusion.keep_ref
  41.1 0.2 shard_map.42
  41.3 2.4 %collective-permute-start.2 = (bf16[28,64,128]{2,1,0:T(8,128)(2,1)S(1)}, bf16[28,64,128]{2,1,0:T(8,128)(2,1)}, u32[]{:S(2)}, u32[]{:S(2)}) collective-permute-start(bf16[28,64,128]{2,1,0:T(8,128)(2,1)S(1)} %shard_map.42), channel_id=1, source_target_pairs={{8,16},{24,32},{40,48},{56,64},{72,80},{88,96},{104,112},{120,128}... | collective-permute-start | bytes 1376264 | tf_op jit(solution)/shard_map/ppermute | solution.py:390
  43.7 0.0 collective-permute-done.1.mate_ref
  43.7 3.7 %shard_map.40 = (f32[64,512]{1,0:T(8,128)S(1)}, f32[48,64,128]{2,1,0:T(8,128)S(1)}) custom-call(bf16[52,64,128]{2,1,0:T(8,128)(2,1)S(1)} %collective-permute-done.1.mate_ref, bf16[52,64,128]{2,1,0:T(8,128)(2,1)S(1)} %copy_bitcast_fusion.own_ref, bf16[3,256,256]{2,1,0:T(8,128)(2,1)S(1)} %get-tuple-element.13.w_ref), custom_call_target="tpu_custom_call" | custom-call | flops 3000000000 | bytes 3000000 | tf_op jit(solution)/shard_map/pallas_call | solution.py:201
  47.4 0.1 collective-permute-done.near_ref
  47.5 2.6 %shard_map.41 = f32[32,8,128]{2,1,0:T(8,128)} custom-call(bf16[28,64,128]{2,1,0:T(8,128)(2,1)S(1)} %collective-permute-done.near_ref, f32[48,64,128]{2,1,0:T(8,128)S(1)} %get-tuple-element.14.late_ref, f32[64,512]{1,0:T(8,128)S(1)} %get-tuple-element.15.first_ref, bf16[384,256]{1,0:T(8,128)(2,1)S(1)} %get-tuple-element.16.w_ref), custom_call_target="tpu_custom_call" | custom-call | flops 2000000000 | bytes 3000000 | tf_op jit(solution)/shard_map/pallas_call | solution.py:211
  50.2 9.1 %all-to-all-start.1 = ((f32[32,8,128]{2,1,0:T(8,128)}), f32[32,8,128]{2,1,0:T(8,128)S(1)}, u32[]{:S(2)}, u32[]{:S(2)}) async-start(f32[32,8,128]{2,1,0:T(8,128)} %shard_map.41), calls=%async_computation.1 | async-start | bytes 262144 | tf_op jit(solution)/shard_map/all_to_all | solution.py:404
  59.3 0.0 collective-permute-done.2.far_ref
  59.3 0.0 copy-start.2
  59.3 4.4 %shard_map.43.v_in = bf16[50,64,256]{2,1,0:T(8,128)(2,1)} custom-call(bf16[28,64,128]{2,1,0:T(8,128)(2,1)S(1)} %collective-permute-done.near_ref, bf16[28,64,128]{2,1,0:T(8,128)(2,1)} %collective-permute-done.2.far_ref, bf16[52,64,128]{2,1,0:T(8,128)(2,1)S(1)} %copy_bitcast_fusion.own_ref, bf16[52,64,128]{2,1,0:T(8,128)(2,1)S(1)} %collective-permute-done.1.mate_ref, ...), custom_call_target="tpu_custom_call" | custom-call | flops 2000000000 | bytes 4000000 | tf_op jit(solution)/shard_map/pallas_call | solution.py:241
  63.7 3.3 %all-to-all-done.1.parts_ref = f32[32,8,128]{2,1,0:T(8,128)S(1)} async-done(((f32[32,8,128]{2,1,0:T(8,128)}), f32[32,8,128]{2,1,0:T(8,128)S(1)}, u32[]{:S(2)}, u32[]{:S(2)}) %all-to-all-start.1) | async-done | bytes 131104 | tf_op jit(solution)/shard_map/all_to_all | solution.py:404
  67.0 9.2 %all_to_all.26.parts_ref = f32[8,8,128]{2,1,0:T(8,128)S(1)} all-to-all(f32[8,8,128]{2,1,0:T(8,128)S(1)} %shard_map.44), channel_id=1, replica_groups=mesh['x'=4,'y'=4,'core'=2,'mem'=8] {'mem'}, dimensions={0} | all-to-all | bytes 65536 | tf_op jit(solution)/shard_map/all_to_all | solution.py:407
  76.3 0.2 shard_map.45
  76.5 12.4 %all_to_all.27.attn_ref = bf16[32,8,128]{2,1,0:T(8,128)(2,1)S(1)} all-to-all(bf16[32,8,128]{2,1,0:T(8,128)(2,1)S(1)} %shard_map.45), channel_id=1, replica_groups=mesh['x'=4,'y'=4,'core'=2,'mem'=8] {'x','y','core'}, dimensions={0} | all-to-all | bytes 131072 | tf_op jit(solution)/shard_map/all_to_all | solution.py:409
  88.9 4.1 %shard_map.46 = bf16[48,64,128]{2,1,0:T(8,128)(2,1)S(1)} custom-call(bf16[32,8,128]{2,1,0:T(8,128)(2,1)S(1)} %all_to_all.27.attn_ref, bf16[50,64,256]{2,1,0:T(8,128)(2,1)} %shard_map.43.v_in, bf16[52,64,128]{2,1,0:T(8,128)(2,1)S(1)} %copy_bitcast_fusion.own_ref, bf16[3,256,128]{2,1,0:T(8,128)(2,1)S(1)} %copy-done.2), custom_call_target="tpu_custom_call" | custom-call | flops 4000000000 | bytes 4000000 | tf_op jit(solution)/shard_map/pallas_call | solution.py:294
  93.0 0.1 copy_bitcast_fusion.1
  93.1 26.0 %all_to_all.28 = bf16[8,48,8,128]{3,2,1,0:T(8,128)(2,1)S(1)} all-to-all(bf16[8,48,8,128]{3,2,1,0:T(8,128)(2,1)S(1)} %copy_bitcast_fusion.1), channel_id=1, replica_groups=mesh['x'=4,'y'=4,'core'=2,'mem'=8] {'mem'}, dimensions={0} | all-to-all | bytes 1572864 | tf_op jit(solution)/shard_map/all_to_all | solution.py:412
  119.1 1.7 %shard_map.47 = bf16[8,64,2,384]{3,2,1,0:T(2,128)(2,1)} custom-call(bf16[8,384,128]{2,1,0:T(8,128)(2,1)S(1)} %bitcast.19), custom_call_target="tpu_custom_call" | custom-call | bytes 1600000 | tf_op jit(solution)/shard_map/pallas_call | solution.py:365
  (7 shorter events, 0.1 us)
Async XLA Ops:
  1.7 34.8 %copy-start.3 = (bf16[9,64,64]{2,1,0:T(8,128)(2,1)S(1)}, bf16[9,64,64]{2,1,0:T(8,128)(2,1)}, u32[]{:S(2)}) copy-start(bf16[9,64,64]{2,1,0:T(8,128)(2,1)} %param.5) | copy-start | bytes 221188
  1.8 34.9 %copy-start = (bf16[9,192,64]{1,2,0:T(8,128)(2,1)S(1)}, bf16[9,192,64]{1,2,0:T(8,128)(2,1)}, u32[]{:S(2)}) copy-start(bf16[9,192,64]{1,2,0:T(8,128)(2,1)} %param.4) | copy-start | bytes 663556
  34.0 9.7 %collective-permute-start.1 = (bf16[52,64,128]{2,1,0:T(8,128)(2,1)S(1)}, bf16[52,64,128]{2,1,0:T(8,128)(2,1)S(1)}, u32[]{:S(2)}, u32[]{:S(2)}) collective-permute-start(bf16[52,64,128]{2,1,0:T(8,128)(2,1)S(1)} %copy_bitcast_fusion.own_ref), channel_id=1, source_target_pairs={{0,8},{8,0},{1,9},{9,1},{2,10},{10,2},{3,11},{11,3},{4,12},{12,4},... | collective-permute-start | bytes 2555912 | tf_op jit(solution)/shard_map/ppermute | solution.py:389
  37.5 3.4 %copy-start.1 = (bf16[3,256,128]{2,1,0:T(8,128)(2,1)}, bf16[3,256,128]{2,1,0:T(8,128)(2,1)S(1)}, u32[]{:S(2)}) copy-start(bf16[3,256,128]{2,1,0:T(8,128)(2,1)S(1)} %get-tuple-element.20.w_ref) | copy-start | bytes 589828
  37.7 9.8 %collective-permute-start = (bf16[28,64,128]{2,1,0:T(8,128)(2,1)S(1)}, bf16[28,64,128]{2,1,0:T(8,128)(2,1)S(1)}, u32[]{:S(2)}, u32[]{:S(2)}) collective-permute-start(bf16[28,64,128]{2,1,0:T(8,128)(2,1)S(1)} %shard_map.38), channel_id=1, source_target_pairs={{8,16},{24,32},{40,48},{56,64},{72,80},{88,96},{104,112},{120,128}... | collective-permute-start | bytes 1376264 | tf_op jit(solution)/shard_map/ppermute | solution.py:388
  41.3 18.0 %collective-permute-start.2 = (bf16[28,64,128]{2,1,0:T(8,128)(2,1)S(1)}, bf16[28,64,128]{2,1,0:T(8,128)(2,1)}, u32[]{:S(2)}, u32[]{:S(2)}) collective-permute-start(bf16[28,64,128]{2,1,0:T(8,128)(2,1)S(1)} %shard_map.42), channel_id=1, source_target_pairs={{8,16},{24,32},{40,48},{56,64},{72,80},{88,96},{104,112},{120,128}... | collective-permute-start | bytes 1376264 | tf_op jit(solution)/shard_map/ppermute | solution.py:390
  50.2 16.8 %all-to-all-start.1 = ((f32[32,8,128]{2,1,0:T(8,128)}), f32[32,8,128]{2,1,0:T(8,128)S(1)}, u32[]{:S(2)}, u32[]{:S(2)}) async-start(f32[32,8,128]{2,1,0:T(8,128)} %shard_map.41), calls=%async_computation.1 | async-start | bytes 262144 | tf_op jit(solution)/shard_map/all_to_all | solution.py:404
  59.3 29.6 %copy-start.2 = (bf16[3,256,128]{2,1,0:T(8,128)(2,1)S(1)}, bf16[3,256,128]{2,1,0:T(8,128)(2,1)}, u32[]{:S(2)}) copy-start(bf16[3,256,128]{2,1,0:T(8,128)(2,1)} %copy-done.1) | copy-start | bytes 589828

commit v4 on v3

--- a/solution.py
+++ b/solution.py
@@ -165,25 +165,42 @@
     return lax.dot_general(q, km, (((1,), (1,)), ((), ())), preferred_element_type=F32)
 
 
+def score_step_by_half(qk, count):
+    lane = lax.broadcasted_iota(jnp.int32, (1, LANES), 1)
+    masks = [(lane % (C // 2) // HD == h).astype(BF) for h in range(HEADS // 2)]
+    parts = []
+    for start in (0, C // 2):
+        q = jnp.concatenate([qk[l, :, start:start + C // 2] for l in range(count)], axis=-1)
+        k = jnp.concatenate([qk[l, :, C + start:C + start + C // 2] for l in range(count)], axis=-1)
+        tiles = [k[:, i * LANES:(i + 1) * LANES] for i in range(count // 4)]
+        km = jnp.concatenate([jnp.concatenate([t * mask for t in tiles], axis=-1) for mask in masks], axis=0)
+        parts.append(lax.dot_general(q, km, (((1,), (1,)), ((), ())), preferred_element_type=F32))
+    return jnp.concatenate(parts, axis=-1)
+
+
 def early_kernel(mate_ref, own_ref, w_ref, s_ref, late_ref):
-    step = 8
+    step, joined = 8, 3
     total = None
-    for i in range(LB // step):
-        start = i * step
+    held = []
+    for start in range(0, LB, step):
         window = slice(start + 1, start + step + 3)
         x = jnp.concatenate([mate_ref[window], own_ref[window]], axis=-1)
         qk = conv_rows(x, w_ref, step)
         late_ref[start:start + step] = qk[:, LANES:].reshape(step, M, LANES)
-        part = score_step(qk[:, :LANES].astype(BF).reshape(step, M, LANES), step)
-        total = part if total is None else total + part
+        held.append(qk[:, :LANES].astype(BF).reshape(step, M, LANES))
+        if len(held) == joined:
+            part = score_step(jnp.concatenate(held, axis=0), step * joined)
+            total = part if total is None else total + part
+            held = []
     s_ref[...] = total
 
 
-def late_kernel(near_ref, late_ref, first_ref, w_ref, s_ref):
-    step = 12
+def late_kernel(near_ref, late_ref, first_ref, w_ref, s_ref, near_out, sems):
+    copy = pltpu.make_async_copy(near_ref, near_out, sems.at[0])
+    copy.start()
+    step = 6
     total = first_ref[...]
-    for i in range(HALF // step):
-        start = i * step
+    for start in range(0, HALF, step):
         x = jnp.concatenate([near_ref[start + 1 + b:start + 1 + b + step] for b in range(3)], axis=-1)
         add = jnp.dot(x.reshape(step * M, 6 * C), w_ref[...], preferred_element_type=F32)
         halves = []
@@ -191,10 +208,11 @@
             at = half * HALF + start
             qk = late_ref[at:at + step].reshape(step * M, LANES) + add[:, half * LANES:(half + 1) * LANES]
             halves.append(qk.astype(BF).reshape(step, M, LANES))
-        total = total + score_step(jnp.concatenate(halves, axis=0), 2 * step)
+        total = total + score_step_by_half(jnp.concatenate(halves, axis=0), 2 * step)
     for a in range(M // 8):
         for b in range(HEADS * M // 128):
             s_ref[a * (HEADS * M // 128) + b] = total[8 * a:8 * (a + 1), 128 * b:128 * (b + 1)]
+    copy.wait()
 
 
 def early_scores(mate, own, w_qk):
@@ -210,13 +228,23 @@
     tiles = HEADS * M * M // 1024
     return pl.pallas_call(
         late_kernel,
-        out_shape=jax.ShapeDtypeStruct((tiles, 8, 128), F32),
+        out_shape=(jax.ShapeDtypeStruct((tiles, 8, 128), F32), pltpu.HBM(near.shape, BF)),
+        out_specs=(pl.BlockSpec(memory_space=pltpu.VMEM), pl.BlockSpec(memory_space=pltpu.HBM)),
+        scratch_shapes=[pltpu.SemaphoreType.DMA((1,))],
         compiler_params=params(),
         cost_estimate=cost(2_000_000_000, 3000000),
     )(near, late, first, w_near)
 
 
-def values_kernel(near_ref, far_ref, own_ref, mate_ref, w_ref, keep_ref, v_out, x_ref, v_ref, sems):
+def values_kernel(near_in, far_in, own_ref, mate_ref, w_ref, keep_ref, v_out, near_ref, far_ref, x_ref, v_ref, sems):
+    arriving = [
+        pltpu.make_async_copy(near_in, near_ref, sems.at[5]),
+        pltpu.make_async_copy(far_in, far_ref, sems.at[6]),
+    ]
+    for copy in arriving:
+        copy.start()
+    for copy in arriving:
+        copy.wait()
     half = LW // 2
     skip = half - (LW - PACK)
     x_ref[:half, :, :LANES] = jnp.concatenate([near_ref[:half, :, :C], far_ref[:half, :, :C]], axis=-1)
@@ -238,27 +266,28 @@
 
 
 def value_maps(near, far, own, mate, w_v, keep):
+    vmem = pl.BlockSpec(memory_space=pltpu.VMEM)
+    hbm = pl.BlockSpec(memory_space=pltpu.HBM)
     return pl.pallas_call(
         values_kernel,
+        in_specs=[hbm, hbm, vmem, vmem, vmem, vmem],
         out_shape=pltpu.HBM((LV, M, 4 * C), BF),
-        out_specs=pl.BlockSpec(memory_space=pltpu.HBM),
+        out_specs=hbm,
         scratch_shapes=[
+            pltpu.VMEM((PACK, M, LANES), BF),
+            pltpu.VMEM((PACK, M, LANES), BF),
             pltpu.VMEM((LW, M, LANES), BF),
             pltpu.VMEM((LV, M, 4 * C), BF),
-            pltpu.SemaphoreType.DMA((5,)),
+            pltpu.SemaphoreType.DMA((7,)),
         ],
         compiler_params=params(),
         cost_estimate=cost(2_000_000_000, 4000000),
-    )(near, far, own, mate, w_v, keep)
+    )(pltpu.with_memory_space_constraint(near, pltpu.HBM), pltpu.with_memory_space_constraint(far, pltpu.HBM), own, mate, w_v, keep)
 
 
 def mix_kernel(attn_ref, v_in, own_ref, w_ref, out_ref, v_ref, att_ref, sems):
-    pieces = 5
-    size = LV // pieces
-    copies = [
-        pltpu.make_async_copy(v_in.at[i * size:(i + 1) * size], v_ref.at[i * size:(i + 1) * size], sems.at[i])
-        for i in range(pieces)
-    ]
+    pieces = (slice(0, 10), slice(10, LV))
+    copies = [pltpu.make_async_copy(v_in.at[p], v_ref.at[p], sems.at[i]) for i, p in enumerate(pieces)]
     for copy in copies:
         copy.start()
     lane = lax.broadcasted_iota(jnp.int32, (1, 4 * C), 1) % LANES
@@ -268,9 +297,9 @@
         [jnp.concatenate([attn_ref[a * lane_tiles + b] for b in range(lane_tiles)], axis=-1) for a in range(M // 8)],
         axis=0,
     )
-    for i in range(pieces):
-        copies[i].wait()
-        for t in range(i * size, (i + 1) * size, 2):
+    for piece, copy in zip(pieces, copies, strict=True):
+        copy.wait()
+        for t in range(piece.start, piece.stop, 2):
             for half in range(2):
                 lanes = slice(half * LANES, (half + 1) * LANES)
                 v = jnp.concatenate([v_ref[t, :, lanes], v_ref[t + 1, :, lanes]], axis=-1)
@@ -298,7 +327,7 @@
         scratch_shapes=[
             pltpu.VMEM((LV, M, 4 * C), BF),
             pltpu.VMEM((LV, M, 4 * C), BF),
-            pltpu.SemaphoreType.DMA((5,)),
+            pltpu.SemaphoreType.DMA((2,)),
         ],
         compiler_params=params(),
         cost_estimate=cost(4_000_000_000, 4000000),
@@ -388,9 +417,10 @@
     near = lax.ppermute(pack(core, own), SPACE, seams)
     mate = lax.ppermute(own, "core", [(0, 1), (1, 0)])
     far = lax.ppermute(pack(1 - core, own), SPACE, seams)
+    own, w_qkv = lax.optimization_barrier((own, w_qkv))
     w_qk, w_near, w_v, w_o = place_weights(core, w_qkv, w_out)
     first, late = early_scores(mate, own, w_qk)
-    part = late_scores(near, late, first, w_near)
+    part, near = late_scores(near, late, first, w_near)
 
     row = lax.broadcasted_iota(jnp.int32, (LV, 1, 4 * C), 2) % (4 * HD) // HD
     lon = lax.broadcasted_iota(jnp.int32, (LV, 1, 4 * C), 0)

time: 121 us -> 120 us (level)
  Pallas kernels: 18.3 us -> 16.2 us
    pallas_call x1, Pallas kernels: 3.7 us -> 2.3 us  [early_scores(): pl.pallas_call(early_kernel, out_shape=(jax.ShapeDtypeStruct((M, HEADS *...]
  transfers between devices with their start and end apart: 4 -> 4, of which waited for: 2 -> 2; matrix products, arithmetic and copies ran while one was open for 0% -> 0% of each run, Pallas kernels for 10% -> 8%
where the time goes in v4:
time: 120 us; the launch traced here: 119 us
  blocking collectives  79.8 us (66%)
  starting transfers between devices  17.2 us (14%)
  Pallas kernels  16.2 us (14%)
  waiting for transfers between devices  3.87 us (3%)
  local copies, waits for them, and re-layouts  1.79 us (1%)
    all_to_all x1, blocking collectives, local(): lax.all_to_all(windows, 'mem', split_axis=0, concat_axis=0, tiled=True)  32 us
    all_to_all x1, blocking collectives, local(): back = lax.all_to_all(mixed, 'mem', split_axis=0, concat_axis=0, tiled=True)  26 us
    all_to_all x1, blocking collectives, local(): attn = lax.all_to_all(attn, SPACE, split_axis=0, concat_axis=0, tiled=True)  12.5 us
    all_to_all x1, blocking collectives, local(): lax.all_to_all(summed(part, GROUPS), 'mem', split_axis=0, concat_axis=0,...  9.24 us
    all_to_all x1, starting transfers between devices, local(): part = lax.all_to_all(part, SPACE, split_axis=0, concat_axis=0, tiled=True)  9.14 us
    pallas_call x1, Pallas kernels, value_maps(): pl.pallas_call(values_kernel, in_specs=[hbm, hbm, vmem, vmem, vmem, vmem]...  4.51 us
    pallas_call x1, Pallas kernels, mix(): pl.pallas_call(mix_kernel, in_specs=[vmem, hbm, vmem, vmem], out_shape=ja...  3.75 us
    all_to_all x1, waiting for transfers between devices, local(): part = lax.all_to_all(part, SPACE, split_axis=0, concat_axis=0, tiled=True)  3.17 us
  transfers between devices with their start and end apart: 4, of which 2 were waited for; matrix products, arithmetic and copies ran while one was open for 0% of the time, Pallas kernels for 8%

profile of v4, /device:TPU:1, one launch (start us, length us, event | category | flops | bytes accessed | tf_op | source)
XLA Modules:
  0.0 119.2 jit_solution(10570935832976289399)
XLA Ops:
  0.0 1.3 %copy.8 = bf16[8,2,64,384]{3,2,1,0:T(8,128)(2,1)S(1)} copy(bf16[8,2,64,384]{3,1,2,0:T(2,128)(2,1)} %bitcast.23) | data formatting | bytes 1572864 | tf_op jit(solution)/shard_map/transpose | solution.py:411
  1.3 0.5 shard_map.37
  1.7 0.0 copy-start.1
  1.8 32.0 %all_to_all.25 = bf16[8,52,8,128]{3,2,1,0:T(8,128)(2,1)S(1)} all-to-all(bf16[8,52,8,128]{3,2,1,0:T(8,128)(2,1)S(1)} %bitcast.18), channel_id=1, replica_groups=mesh['x'=4,'y'=4,'core'=2,'mem'=8] {'mem'}, dimensions={0} | all-to-all | bytes 1703936 | tf_op jit(solution)/shard_map/all_to_all | solution.py:413
  33.7 0.2 copy_bitcast_fusion.own_ref
  34.0 0.0 copy-start
  34.0 2.5 %collective-permute-start.1 = (bf16[52,64,128]{2,1,0:T(8,128)(2,1)S(1)}, bf16[52,64,128]{2,1,0:T(8,128)(2,1)S(1)}, u32[]{:S(2)}, u32[]{:S(2)}) collective-permute-start(bf16[52,64,128]{2,1,0:T(8,128)(2,1)S(1)} %copy_bitcast_fusion.own_ref), channel_id=1, source_target_pairs={{0,8},{8,0},{1,9},{9,1},{2,10},{10,2},{3,11},{11,3},{4,12},{12,4},... | collective-permute-start | bytes 2555912 | tf_op jit(solution)/shard_map/ppermute | solution.py:418
  36.5 0.0 copy-done.1
  36.5 0.1 copy.10
  36.7 0.2 shard_map.38
  36.9 3.1 %collective-permute-start = (bf16[28,64,128]{2,1,0:T(8,128)(2,1)S(1)}, bf16[28,64,128]{2,1,0:T(8,128)(2,1)S(1)}, u32[]{:S(2)}, u32[]{:S(2)}) collective-permute-start(bf16[28,64,128]{2,1,0:T(8,128)(2,1)S(1)} %shard_map.38), channel_id=1, source_target_pairs={{8,16},{24,32},{40,48},{56,64},{72,80},{88,96},{104,112},{120,128}... | collective-permute-start | bytes 1376264 | tf_op jit(solution)/shard_map/ppermute | solution.py:417
  40.0 0.2 or_select_fusion.keep_ref
  40.2 0.2 shard_map.42
  40.4 2.4 %collective-permute-start.2 = (bf16[28,64,128]{2,1,0:T(8,128)(2,1)S(1)}, bf16[28,64,128]{2,1,0:T(8,128)(2,1)}, u32[]{:S(2)}, u32[]{:S(2)}) collective-permute-start(bf16[28,64,128]{2,1,0:T(8,128)(2,1)S(1)} %shard_map.42), channel_id=1, source_target_pairs={{8,16},{24,32},{40,48},{56,64},{72,80},{88,96},{104,112},{120,128}... | collective-permute-start | bytes 1376264 | tf_op jit(solution)/shard_map/ppermute | solution.py:419
  42.9 0.0 copy-done
  42.9 0.8 shard_map.39
  43.7 0.0 collective-permute-done.1.mate_ref
  43.7 2.3 %shard_map.40 = (f32[64,512]{1,0:T(8,128)S(1)}, f32[48,64,128]{2,1,0:T(8,128)S(1)}) custom-call(bf16[52,64,128]{2,1,0:T(8,128)(2,1)S(1)} %collective-permute-done.1.mate_ref, bf16[52,64,128]{2,1,0:T(8,128)(2,1)S(1)} %copy_bitcast_fusion.own_ref, bf16[3,256,256]{2,1,0:T(8,128)(2,1)S(1)} %get-tuple-element.19.w_ref), custom_call_target="tpu_custom_call" | custom-call | flops 3000000000 | bytes 3000000 | tf_op jit(solution)/shard_map/pallas_call | solution.py:219
  46.0 0.7 collective-permute-done.near_ref
  46.7 2.1 %shard_map.41 = (f32[32,8,128]{2,1,0:T(8,128)}, bf16[28,64,128]{2,1,0:T(8,128)(2,1)}) custom-call(bf16[28,64,128]{2,1,0:T(8,128)(2,1)S(1)} %collective-permute-done.near_ref, f32[48,64,128]{2,1,0:T(8,128)S(1)} %get-tuple-element.20.late_ref, f32[64,512]{1,0:T(8,128)S(1)} %get-tuple-element.21.first_ref, bf16[384,256]{1,0:T(8,128)(2,1)S(1)} %get-tuple-element.22.w_ref), custom_call_target="tpu_custom_call" | custom-call | flops 2000000000 | bytes 3000000 | tf_op jit(solution)/shard_map/pallas_call | solution.py:229
  48.8 9.1 %all-to-all-start.1 = ((f32[32,8,128]{2,1,0:T(8,128)}), f32[32,8,128]{2,1,0:T(8,128)S(1)}, u32[]{:S(2)}, u32[]{:S(2)}) async-start(f32[32,8,128]{2,1,0:T(8,128)} %get-tuple-element.23), calls=%async_computation.1 | async-start | bytes 262144 | tf_op jit(solution)/shard_map/all_to_all | solution.py:434
  57.9 0.0 collective-permute-done.2.far_in
  57.9 4.5 %shard_map.43.v_in = bf16[50,64,256]{2,1,0:T(8,128)(2,1)} custom-call(bf16[28,64,128]{2,1,0:T(8,128)(2,1)} %get-tuple-element.24.near_in, bf16[28,64,128]{2,1,0:T(8,128)(2,1)} %collective-permute-done.2.far_in, bf16[52,64,128]{2,1,0:T(8,128)(2,1)S(1)} %copy_bitcast_fusion.own_ref, bf16[52,64,128]{2,1,0:T(8,128)(2,1)S(1)} %collective-permute-done.1.mate_ref, ...), custom_call_target="tpu_custom_call" | custom-call | flops 2000000000 | bytes 4000000 | tf_op jit(solution)/shard_map/pallas_call | solution.py:271
  62.5 3.2 %all-to-all-done.1.parts_ref = f32[32,8,128]{2,1,0:T(8,128)S(1)} async-done(((f32[32,8,128]{2,1,0:T(8,128)}), f32[32,8,128]{2,1,0:T(8,128)S(1)}, u32[]{:S(2)}, u32[]{:S(2)}) %all-to-all-start.1) | async-done | bytes 131104 | tf_op jit(solution)/shard_map/all_to_all | solution.py:434
  65.7 9.2 %all_to_all.26.parts_ref = f32[8,8,128]{2,1,0:T(8,128)S(1)} all-to-all(f32[8,8,128]{2,1,0:T(8,128)S(1)} %shard_map.44), channel_id=1, replica_groups=mesh['x'=4,'y'=4,'core'=2,'mem'=8] {'mem'}, dimensions={0} | all-to-all | bytes 65536 | tf_op jit(solution)/shard_map/all_to_all | solution.py:437
  74.9 0.2 shard_map.45
  75.1 12.5 %all_to_all.27.attn_ref = bf16[32,8,128]{2,1,0:T(8,128)(2,1)S(1)} all-to-all(bf16[32,8,128]{2,1,0:T(8,128)(2,1)S(1)} %shard_map.45), channel_id=1, replica_groups=mesh['x'=4,'y'=4,'core'=2,'mem'=8] {'x','y','core'}, dimensions={0} | all-to-all | bytes 131072 | tf_op jit(solution)/shard_map/all_to_all | solution.py:439
  87.6 3.7 %shard_map.46 = bf16[48,64,128]{2,1,0:T(8,128)(2,1)S(1)} custom-call(bf16[32,8,128]{2,1,0:T(8,128)(2,1)S(1)} %all_to_all.27.attn_ref, bf16[50,64,256]{2,1,0:T(8,128)(2,1)} %shard_map.43.v_in, bf16[52,64,128]{2,1,0:T(8,128)(2,1)S(1)} %copy_bitcast_fusion.own_ref, bf16[3,256,128]{2,1,0:T(8,128)(2,1)S(1)} %get-tuple-element.28.w_ref), custom_call_target="tpu_custom_call" | custom-call | flops 4000000000 | bytes 4000000 | tf_op jit(solution)/shard_map/pallas_call | solution.py:323
  91.4 0.1 copy_bitcast_fusion.1
  91.5 26.0 %all_to_all.28 = bf16[8,48,8,128]{3,2,1,0:T(8,128)(2,1)S(1)} all-to-all(bf16[8,48,8,128]{3,2,1,0:T(8,128)(2,1)S(1)} %copy_bitcast_fusion.1), channel_id=1, replica_groups=mesh['x'=4,'y'=4,'core'=2,'mem'=8] {'mem'}, dimensions={0} | all-to-all | bytes 1572864 | tf_op jit(solution)/shard_map/all_to_all | solution.py:442
  117.5 1.7 %shard_map.47 = bf16[8,64,2,384]{3,2,1,0:T(2,128)(2,1)} custom-call(bf16[8,384,128]{2,1,0:T(8,128)(2,1)S(1)} %bitcast.19), custom_call_target="tpu_custom_call" | custom-call | bytes 1600000 | tf_op jit(solution)/shard_map/pallas_call | solution.py:394
  (4 shorter events, 0.1 us)
Async XLA Ops:
  1.7 34.8 %copy-start.1 = (bf16[9,64,64]{2,1,0:T(8,128)(2,1)S(1)}, bf16[9,64,64]{2,1,0:T(8,128)(2,1)}, u32[]{:S(2)}) copy-start(bf16[9,64,64]{2,1,0:T(8,128)(2,1)} %param.5) | copy-start | bytes 221188
  34.0 8.9 %copy-start = (bf16[9,192,64]{1,2,0:T(8,128)(2,1)S(1)}, bf16[9,192,64]{1,2,0:T(8,128)(2,1)}, u32[]{:S(2)}) copy-start(bf16[9,192,64]{1,2,0:T(8,128)(2,1)} %param.4) | copy-start | bytes 663556
  34.0 9.7 %collective-permute-start.1 = (bf16[52,64,128]{2,1,0:T(8,128)(2,1)S(1)}, bf16[52,64,128]{2,1,0:T(8,128)(2,1)S(1)}, u32[]{:S(2)}, u32[]{:S(2)}) collective-permute-start(bf16[52,64,128]{2,1,0:T(8,128)(2,1)S(1)} %copy_bitcast_fusion.own_ref), channel_id=1, source_target_pairs={{0,8},{8,0},{1,9},{9,1},{2,10},{10,2},{3,11},{11,3},{4,12},{12,4},... | collective-permute-start | bytes 2555912 | tf_op jit(solution)/shard_map/ppermute | solution.py:418
  36.9 9.8 %collective-permute-start = (bf16[28,64,128]{2,1,0:T(8,128)(2,1)S(1)}, bf16[28,64,128]{2,1,0:T(8,128)(2,1)S(1)}, u32[]{:S(2)}, u32[]{:S(2)}) collective-permute-start(bf16[28,64,128]{2,1,0:T(8,128)(2,1)S(1)} %shard_map.38), channel_id=1, source_target_pairs={{8,16},{24,32},{40,48},{56,64},{72,80},{88,96},{104,112},{120,128}... | collective-permute-start | bytes 1376264 | tf_op jit(solution)/shard_map/ppermute | solution.py:417
  40.4 17.5 %collective-permute-start.2 = (bf16[28,64,128]{2,1,0:T(8,128)(2,1)S(1)}, bf16[28,64,128]{2,1,0:T(8,128)(2,1)}, u32[]{:S(2)}, u32[]{:S(2)}) collective-permute-start(bf16[28,64,128]{2,1,0:T(8,128)(2,1)S(1)} %shard_map.42), channel_id=1, source_target_pairs={{8,16},{24,32},{40,48},{56,64},{72,80},{88,96},{104,112},{120,128}... | collective-permute-start | bytes 1376264 | tf_op jit(solution)/shard_map/ppermute | solution.py:419
  48.8 16.9 %all-to-all-start.1 = ((f32[32,8,128]{2,1,0:T(8,128)}), f32[32,8,128]{2,1,0:T(8,128)S(1)}, u32[]{:S(2)}, u32[]{:S(2)}) async-start(f32[32,8,128]{2,1,0:T(8,128)} %get-tuple-element.23), calls=%async_computation.1 | async-start | bytes 262144 | tf_op jit(solution)/shard_map/all_to_all | solution.py:434

commit v5 on v4

--- a/solution.py
+++ b/solution.py
@@ -22,6 +22,7 @@
 LV = LB + 2
 HALF = LB // 2
 PACK = HALF + 4
+HELD = 20
 SPACE = ("x", "y", "core")
 BF = jnp.bfloat16
 F32 = jnp.float32
@@ -236,7 +237,7 @@
     )(near, late, first, w_near)
 
 
-def values_kernel(near_in, far_in, own_ref, mate_ref, w_ref, keep_ref, v_out, near_ref, far_ref, x_ref, v_ref, sems):
+def values_kernel(near_in, far_in, own_ref, mate_ref, w_ref, keep_ref, held_ref, v_out, near_ref, far_ref, x_ref, v_ref, sems):
     arriving = [
         pltpu.make_async_copy(near_in, near_ref, sems.at[5]),
         pltpu.make_async_copy(far_in, far_ref, sems.at[6]),
@@ -257,10 +258,14 @@
             [ref[start + b:start + b + step] for b in range(3) for ref in (x_ref, own_ref, mate_ref)], axis=-1
         )
         v = jnp.dot(x.reshape(step * M, 18 * C), w, preferred_element_type=F32)
-        piece = slice(start, start + step)
-        v_ref[piece] = (v.reshape(step, M, 4 * C) * keep_ref[piece]).astype(BF)
-        copies.append(pltpu.make_async_copy(v_ref.at[piece], v_out.at[piece], sems.at[start // step]))
-        copies[-1].start()
+        v = (v.reshape(step, M, 4 * C) * keep_ref[start:start + step]).astype(BF)
+        if start < HELD:
+            held_ref[start:start + step] = v
+        else:
+            piece = slice(start - HELD, start - HELD + step)
+            v_ref[piece] = v
+            copies.append(pltpu.make_async_copy(v_ref.at[piece], v_out.at[piece], sems.at[start // step]))
+            copies[-1].start()
     for copy in copies:
         copy.wait()
 
@@ -271,13 +276,13 @@
     return pl.pallas_call(
         values_kernel,
         in_specs=[hbm, hbm, vmem, vmem, vmem, vmem],
-        out_shape=pltpu.HBM((LV, M, 4 * C), BF),
-        out_specs=hbm,
+        out_shape=(jax.ShapeDtypeStruct((HELD, M, 4 * C), BF), pltpu.HBM((LV - HELD, M, 4 * C), BF)),
+        out_specs=(vmem, hbm),
         scratch_shapes=[
             pltpu.VMEM((PACK, M, LANES), BF),
             pltpu.VMEM((PACK, M, LANES), BF),
             pltpu.VMEM((LW, M, LANES), BF),
-            pltpu.VMEM((LV, M, 4 * C), BF),
+            pltpu.VMEM((LV - HELD, M, 4 * C), BF),
             pltpu.SemaphoreType.DMA((7,)),
         ],
         compiler_params=params(),
@@ -285,11 +290,9 @@
     )(pltpu.with_memory_space_constraint(near, pltpu.HBM), pltpu.with_memory_space_constraint(far, pltpu.HBM), own, mate, w_v, keep)
 
 
-def mix_kernel(attn_ref, v_in, own_ref, w_ref, out_ref, v_ref, att_ref, sems):
-    pieces = (slice(0, 10), slice(10, LV))
-    copies = [pltpu.make_async_copy(v_in.at[p], v_ref.at[p], sems.at[i]) for i, p in enumerate(pieces)]
-    for copy in copies:
-        copy.start()
+def mix_kernel(attn_ref, held_ref, v_in, own_ref, w_ref, out_ref, v_ref, att_ref, sems):
+    copy = pltpu.make_async_copy(v_in, v_ref, sems.at[0])
+    copy.start()
     lane = lax.broadcasted_iota(jnp.int32, (1, 4 * C), 1) % LANES
     masks = [(lane // (4 * HD) == h).astype(BF) for h in range(HEADS // 2)]
     lane_tiles = HEADS * M // 128
@@ -297,12 +300,14 @@
         [jnp.concatenate([attn_ref[a * lane_tiles + b] for b in range(lane_tiles)], axis=-1) for a in range(M // 8)],
         axis=0,
     )
-    for piece, copy in zip(pieces, copies, strict=True):
-        copy.wait()
-        for t in range(piece.start, piece.stop, 2):
+    for first, ref in ((0, held_ref), (HELD, v_ref)):
+        if first:
+            copy.wait()
+        for i in range(0, ref.shape[0], 2):
+            t = first + i
             for half in range(2):
                 lanes = slice(half * LANES, (half + 1) * LANES)
-                v = jnp.concatenate([v_ref[t, :, lanes], v_ref[t + 1, :, lanes]], axis=-1)
+                v = jnp.concatenate([ref[i, :, lanes], ref[i + 1, :, lanes]], axis=-1)
                 vm = jnp.concatenate([v * mask for mask in masks], axis=0)
                 weights = attn[:, half * 4 * M:(half + 1) * 4 * M]
                 blended = jnp.dot(weights, vm, preferred_element_type=F32).astype(BF)
@@ -317,21 +322,21 @@
         out_ref[start:start + step] = total.astype(BF).reshape(step, M, LANES)
 
 
-def mix(attn, v, own, w_o):
+def mix(attn, held, v, own, w_o):
     vmem = pl.BlockSpec(memory_space=pltpu.VMEM)
     hbm = pl.BlockSpec(memory_space=pltpu.HBM)
     return pl.pallas_call(
         mix_kernel,
-        in_specs=[vmem, hbm, vmem, vmem],
+        in_specs=[vmem, vmem, hbm, vmem, vmem],
         out_shape=jax.ShapeDtypeStruct((LB, M, LANES), BF),
         scratch_shapes=[
+            pltpu.VMEM((LV - HELD, M, 4 * C), BF),
             pltpu.VMEM((LV, M, 4 * C), BF),
-            pltpu.VMEM((LV, M, 4 * C), BF),
-            pltpu.SemaphoreType.DMA((2,)),
+            pltpu.SemaphoreType.DMA((1,)),
         ],
         compiler_params=params(),
         cost_estimate=cost(4_000_000_000, 4000000),
-    )(attn, pltpu.with_memory_space_constraint(v, pltpu.HBM), own, w_o)
+    )(attn, held, pltpu.with_memory_space_constraint(v, pltpu.HBM), own, w_o)
 
 
 def total_kernel(parts_ref, out_ref):
@@ -378,23 +383,41 @@
     )(parts)
 
 
-def final_kernel(back_ref, out_ref, cells_ref):
+def row_order():
+    old = lax.broadcasted_iota(jnp.int32, (LANES, LANES), 0)
+    new = lax.broadcasted_iota(jnp.int32, (LANES, LANES), 1)
+    return (old % ROWS * C + old // ROWS == new).astype(BF)
+
+
+def final_kernel(back_ref, out_hbm, cells_ref, out_ref, sems):
     members = out_ref.shape[0]
     count = LB * members
     for g in range(GROUPS):
         cells_ref[g * count:(g + 1) * count] = back_ref[g].astype(F32)
+    order = row_order()
+    copies = []
     for m in range(members):
-        rows = cells_ref[pl.ds(m, LON, stride=members)].T
-        for r in range(ROWS):
-            out_ref[m, :, r] = rows[r * C:(r + 1) * C].astype(BF)
+        cells = cells_ref[pl.ds(m, LON, stride=members)].astype(BF)
+        rows = lax.dot_general(order, cells, (((1,), (1,)), ((), ())), preferred_element_type=F32)
+        out_ref[m] = rows.astype(BF).reshape(C, ROWS, LON)
+        copies.append(pltpu.make_async_copy(out_ref.at[m], out_hbm.at[m], sems.at[m]))
+        copies[m].start()
+    for copy in copies:
+        copy.wait()
 
 
 def final_layout(back):
     members = back.shape[1] // LB
+    shape = (members, C, ROWS, LON)
     return pl.pallas_call(
         final_kernel,
-        out_shape=jax.ShapeDtypeStruct((members, C, ROWS, LON), BF),
-        scratch_shapes=[pltpu.VMEM((LON * members, LANES), F32)],
+        out_shape=jax.ShapeDtypeStruct(shape, BF),
+        out_specs=pl.BlockSpec(memory_space=pl.ANY),
+        scratch_shapes=[
+            pltpu.VMEM((LON * members, LANES), F32),
+            pltpu.VMEM(shape, BF),
+            pltpu.SemaphoreType.DMA((members,)),
+        ],
         compiler_params=params(),
         cost_estimate=cost(0, 1600000),
     )(back)
@@ -432,12 +455,12 @@
     )
     keep = jnp.where(outside, 0.0, 1.0).astype(F32)
     part = lax.all_to_all(part, SPACE, split_axis=0, concat_axis=0, tiled=True)
-    v = value_maps(near, far, own, mate, w_v, keep)
-    part, v = lax.optimization_barrier((part, v))
+    held, v = value_maps(near, far, own, mate, w_v, keep)
+    part, held, v = lax.optimization_barrier((part, held, v))
     part = lax.all_to_all(summed(part, GROUPS), "mem", split_axis=0, concat_axis=0, tiled=True)
     attn = softmax_of(part, 1.0 / math.sqrt(HD * ROWS * places * LON), places)
     attn = lax.all_to_all(attn, SPACE, split_axis=0, concat_axis=0, tiled=True)
-    mixed = mix(attn, v, own, w_o)
+    mixed = mix(attn, held, v, own, w_o)
     mixed = jnp.transpose(mixed.reshape(LB, GROUPS, members_here, LANES), (1, 0, 2, 3))
     back = lax.all_to_all(mixed, "mem", split_axis=0, concat_axis=0, tiled=True)
     return final_layout(back.reshape(GROUPS, LB * members_here, LANES))

time: 120 us -> 119 us (level)
  no operation moved by 1% of the time
where the time goes in v5:
time: 119 us
  blocking collectives  79.7 us (67%)
  starting transfers between devices  17.2 us (14%)
  Pallas kernels  15.8 us (13%)
  waiting for transfers between devices  3.95 us (3%)
  local copies, waits for them, and re-layouts  1.79 us (2%)
    all_to_all x1, blocking collectives, local(): lax.all_to_all(windows, 'mem', split_axis=0, concat_axis=0, tiled=True)  32 us
    all_to_all x1, blocking collectives, local(): back = lax.all_to_all(mixed, 'mem', split_axis=0, concat_axis=0, tiled=True)  26 us
    all_to_all x1, blocking collectives, local(): attn = lax.all_to_all(attn, SPACE, split_axis=0, concat_axis=0, tiled=True)  12.5 us
    all_to_all x1, blocking collectives, local(): lax.all_to_all(summed(part, GROUPS), 'mem', split_axis=0, concat_axis=0,...  9.24 us
    all_to_all x1, starting transfers between devices, local(): part = lax.all_to_all(part, SPACE, split_axis=0, concat_axis=0, tiled=True)  9.14 us
    pallas_call x1, Pallas kernels, value_maps(): pl.pallas_call(values_kernel, in_specs=[hbm, hbm, vmem, vmem, vmem, vmem]...  4.43 us
    pallas_call x1, Pallas kernels, mix(): pl.pallas_call(mix_kernel, in_specs=[vmem, vmem, hbm, vmem, vmem], out_sh...  3.69 us
    all_to_all x1, waiting for transfers between devices, local(): part = lax.all_to_all(part, SPACE, split_axis=0, concat_axis=0, tiled=True)  3.25 us
  transfers between devices with their start and end apart: 4, of which 2 were waited for; matrix products, arithmetic and copies ran while one was open for 0% of the time, Pallas kernels for 8%

profile of v5, /device:TPU:1, one launch (start us, length us, event | category | flops | bytes accessed | tf_op | source)
XLA Modules:
  0.0 118.8 jit_solution(5172519705033105361)
XLA Ops:
  0.0 1.3 %copy.8 = bf16[8,2,64,384]{3,2,1,0:T(8,128)(2,1)S(1)} copy(bf16[8,2,64,384]{3,1,2,0:T(2,128)(2,1)} %bitcast.23) | data formatting | bytes 1572864 | tf_op jit(solution)/shard_map/transpose | solution.py:434
  1.3 0.5 shard_map.37
  1.7 0.0 copy-start.1
  1.8 32.0 %all_to_all.25 = bf16[8,52,8,128]{3,2,1,0:T(8,128)(2,1)S(1)} all-to-all(bf16[8,52,8,128]{3,2,1,0:T(8,128)(2,1)S(1)} %bitcast.18), channel_id=1, replica_groups=mesh['x'=4,'y'=4,'core'=2,'mem'=8] {'mem'}, dimensions={0} | all-to-all | bytes 1703936 | tf_op jit(solution)/shard_map/all_to_all | solution.py:436
  33.7 0.2 copy_bitcast_fusion.own_ref
  34.0 0.0 copy-start
  34.0 2.5 %collective-permute-start.1 = (bf16[52,64,128]{2,1,0:T(8,128)(2,1)S(1)}, bf16[52,64,128]{2,1,0:T(8,128)(2,1)S(1)}, u32[]{:S(2)}, u32[]{:S(2)}) collective-permute-start(bf16[52,64,128]{2,1,0:T(8,128)(2,1)S(1)} %copy_bitcast_fusion.own_ref), channel_id=1, source_target_pairs={{0,8},{8,0},{1,9},{9,1},{2,10},{10,2},{3,11},{11,3},{4,12},{12,4},... | collective-permute-start | bytes 2555912 | tf_op jit(solution)/shard_map/ppermute | solution.py:441
  36.5 0.0 copy-done.1
  36.5 0.1 copy.10
  36.7 0.2 shard_map.38
  36.9 3.1 %collective-permute-start = (bf16[28,64,128]{2,1,0:T(8,128)(2,1)S(1)}, bf16[28,64,128]{2,1,0:T(8,128)(2,1)S(1)}, u32[]{:S(2)}, u32[]{:S(2)}) collective-permute-start(bf16[28,64,128]{2,1,0:T(8,128)(2,1)S(1)} %shard_map.38), channel_id=1, source_target_pairs={{8,16},{24,32},{40,48},{56,64},{72,80},{88,96},{104,112},{120,128}... | collective-permute-start | bytes 1376264 | tf_op jit(solution)/shard_map/ppermute | solution.py:440
  40.0 0.2 or_select_fusion.keep_ref
  40.2 0.2 shard_map.42
  40.4 2.4 %collective-permute-start.2 = (bf16[28,64,128]{2,1,0:T(8,128)(2,1)S(1)}, bf16[28,64,128]{2,1,0:T(8,128)(2,1)}, u32[]{:S(2)}, u32[]{:S(2)}) collective-permute-start(bf16[28,64,128]{2,1,0:T(8,128)(2,1)S(1)} %shard_map.42), channel_id=1, source_target_pairs={{8,16},{24,32},{40,48},{56,64},{72,80},{88,96},{104,112},{120,128}... | collective-permute-start | bytes 1376264 | tf_op jit(solution)/shard_map/ppermute | solution.py:442
  42.9 0.0 copy-done
  42.9 0.8 shard_map.39
  43.7 0.0 collective-permute-done.1.mate_ref
  43.7 2.3 %shard_map.40 = (f32[64,512]{1,0:T(8,128)S(1)}, f32[48,64,128]{2,1,0:T(8,128)S(1)}) custom-call(bf16[52,64,128]{2,1,0:T(8,128)(2,1)S(1)} %collective-permute-done.1.mate_ref, bf16[52,64,128]{2,1,0:T(8,128)(2,1)S(1)} %copy_bitcast_fusion.own_ref, bf16[3,256,256]{2,1,0:T(8,128)(2,1)S(1)} %get-tuple-element.22.w_ref), custom_call_target="tpu_custom_call" | custom-call | flops 3000000000 | bytes 3000000 | tf_op jit(solution)/shard_map/pallas_call | solution.py:220
  46.0 0.7 collective-permute-done.near_ref
  46.7 2.1 %shard_map.41 = (f32[32,8,128]{2,1,0:T(8,128)}, bf16[28,64,128]{2,1,0:T(8,128)(2,1)}) custom-call(bf16[28,64,128]{2,1,0:T(8,128)(2,1)S(1)} %collective-permute-done.near_ref, f32[48,64,128]{2,1,0:T(8,128)S(1)} %get-tuple-element.23.late_ref, f32[64,512]{1,0:T(8,128)S(1)} %get-tuple-element.24.first_ref, bf16[384,256]{1,0:T(8,128)(2,1)S(1)} %get-tuple-element.25.w_ref), custom_call_target="tpu_custom_call" | custom-call | flops 2000000000 | bytes 3000000 | tf_op jit(solution)/shard_map/pallas_call | solution.py:230
  48.8 9.1 %all-to-all-start.1 = ((f32[32,8,128]{2,1,0:T(8,128)}), f32[32,8,128]{2,1,0:T(8,128)S(1)}, u32[]{:S(2)}, u32[]{:S(2)}) async-start(f32[32,8,128]{2,1,0:T(8,128)} %get-tuple-element.26), calls=%async_computation.1 | async-start | bytes 262144 | tf_op jit(solution)/shard_map/all_to_all | solution.py:457
  57.9 0.0 collective-permute-done.2.far_in
  57.9 4.4 %shard_map.43 = (bf16[20,64,256]{2,1,0:T(8,128)(2,1)S(1)}, bf16[30,64,256]{2,1,0:T(8,128)(2,1)}) custom-call(bf16[28,64,128]{2,1,0:T(8,128)(2,1)} %get-tuple-element.27.near_in, bf16[28,64,128]{2,1,0:T(8,128)(2,1)} %collective-permute-done.2.far_in, bf16[52,64,128]{2,1,0:T(8,128)(2,1)S(1)} %copy_bitcast_fusion.own_ref, ...), custom_call_target="tpu_custom_call" | custom-call | flops 2000000000 | bytes 4000000 | tf_op jit(solution)/shard_map/pallas_call | solution.py:276
  62.4 3.3 %all-to-all-done.1.parts_ref = f32[32,8,128]{2,1,0:T(8,128)S(1)} async-done(((f32[32,8,128]{2,1,0:T(8,128)}), f32[32,8,128]{2,1,0:T(8,128)S(1)}, u32[]{:S(2)}, u32[]{:S(2)}) %all-to-all-start.1) | async-done | bytes 131104 | tf_op jit(solution)/shard_map/all_to_all | solution.py:457
  65.7 9.2 %all_to_all.26.parts_ref = f32[8,8,128]{2,1,0:T(8,128)S(1)} all-to-all(f32[8,8,128]{2,1,0:T(8,128)S(1)} %shard_map.44), channel_id=1, replica_groups=mesh['x'=4,'y'=4,'core'=2,'mem'=8] {'mem'}, dimensions={0} | all-to-all | bytes 65536 | tf_op jit(solution)/shard_map/all_to_all | solution.py:460
  74.9 0.2 shard_map.45
  75.1 12.5 %all_to_all.27.attn_ref = bf16[32,8,128]{2,1,0:T(8,128)(2,1)S(1)} all-to-all(bf16[32,8,128]{2,1,0:T(8,128)(2,1)S(1)} %shard_map.45), channel_id=1, replica_groups=mesh['x'=4,'y'=4,'core'=2,'mem'=8] {'x','y','core'}, dimensions={0} | all-to-all | bytes 131072 | tf_op jit(solution)/shard_map/all_to_all | solution.py:462
  87.5 3.7 %shard_map.46 = bf16[48,64,128]{2,1,0:T(8,128)(2,1)S(1)} custom-call(bf16[32,8,128]{2,1,0:T(8,128)(2,1)S(1)} %all_to_all.27.attn_ref, bf16[20,64,256]{2,1,0:T(8,128)(2,1)S(1)} %get-tuple-element.32.held_ref, bf16[30,64,256]{2,1,0:T(8,128)(2,1)} %get-tuple-element.33.v_in, bf16[52,64,128]{2,1,0:T(8,128)(2,1)S(1)} %copy_bitcast_fusion.own_ref, ...), custom_call_target="tpu_custom_call" | custom-call | flops 4000000000 | bytes 4000000 | tf_op jit(solution)/shard_map/pallas_call | solution.py:328
  91.2 0.1 copy_bitcast_fusion.1
  91.4 26.0 %all_to_all.28 = bf16[8,48,8,128]{3,2,1,0:T(8,128)(2,1)S(1)} all-to-all(bf16[8,48,8,128]{3,2,1,0:T(8,128)(2,1)S(1)} %copy_bitcast_fusion.1), channel_id=1, replica_groups=mesh['x'=4,'y'=4,'core'=2,'mem'=8] {'mem'}, dimensions={0} | all-to-all | bytes 1572864 | tf_op jit(solution)/shard_map/all_to_all | solution.py:465
  117.4 1.4 %shard_map.47 = bf16[8,64,2,384]{3,2,1,0:T(2,128)(2,1)} custom-call(bf16[8,384,128]{2,1,0:T(8,128)(2,1)S(1)} %bitcast.19), custom_call_target="tpu_custom_call" | custom-call | bytes 1600000 | tf_op jit(solution)/shard_map/pallas_call | solution.py:412
  (4 shorter events, 0.1 us)
Async XLA Ops:
  1.7 34.8 %copy-start.1 = (bf16[9,64,64]{2,1,0:T(8,128)(2,1)S(1)}, bf16[9,64,64]{2,1,0:T(8,128)(2,1)}, u32[]{:S(2)}) copy-start(bf16[9,64,64]{2,1,0:T(8,128)(2,1)} %param.5) | copy-start | bytes 221188
  34.0 8.9 %copy-start = (bf16[9,192,64]{1,2,0:T(8,128)(2,1)S(1)}, bf16[9,192,64]{1,2,0:T(8,128)(2,1)}, u32[]{:S(2)}) copy-start(bf16[9,192,64]{1,2,0:T(8,128)(2,1)} %param.4) | copy-start | bytes 663556
  34.0 9.7 %collective-permute-start.1 = (bf16[52,64,128]{2,1,0:T(8,128)(2,1)S(1)}, bf16[52,64,128]{2,1,0:T(8,128)(2,1)S(1)}, u32[]{:S(2)}, u32[]{:S(2)}) collective-permute-start(bf16[52,64,128]{2,1,0:T(8,128)(2,1)S(1)} %copy_bitcast_fusion.own_ref), channel_id=1, source_target_pairs={{0,8},{8,0},{1,9},{9,1},{2,10},{10,2},{3,11},{11,3},{4,12},{12,4},... | collective-permute-start | bytes 2555912 | tf_op jit(solution)/shard_map/ppermute | solution.py:441
  36.9 9.8 %collective-permute-start = (bf16[28,64,128]{2,1,0:T(8,128)(2,1)S(1)}, bf16[28,64,128]{2,1,0:T(8,128)(2,1)S(1)}, u32[]{:S(2)}, u32[]{:S(2)}) collective-permute-start(bf16[28,64,128]{2,1,0:T(8,128)(2,1)S(1)} %shard_map.38), channel_id=1, source_target_pairs={{8,16},{24,32},{40,48},{56,64},{72,80},{88,96},{104,112},{120,128}... | collective-permute-start | bytes 1376264 | tf_op jit(solution)/shard_map/ppermute | solution.py:440
  40.4 17.5 %collective-permute-start.2 = (bf16[28,64,128]{2,1,0:T(8,128)(2,1)S(1)}, bf16[28,64,128]{2,1,0:T(8,128)(2,1)}, u32[]{:S(2)}, u32[]{:S(2)}) collective-permute-start(bf16[28,64,128]{2,1,0:T(8,128)(2,1)S(1)} %shard_map.42), channel_id=1, source_target_pairs={{8,16},{24,32},{40,48},{56,64},{72,80},{88,96},{104,112},{120,128}... | collective-permute-start | bytes 1376264 | tf_op jit(solution)/shard_map/ppermute | solution.py:442
  48.8 16.9 %all-to-all-start.1 = ((f32[32,8,128]{2,1,0:T(8,128)}), f32[32,8,128]{2,1,0:T(8,128)S(1)}, u32[]{:S(2)}, u32[]{:S(2)}) async-start(f32[32,8,128]{2,1,0:T(8,128)} %get-tuple-element.26), calls=%async_computation.1 | async-start | bytes 262144 | tf_op jit(solution)/shard_map/all_to_all | solution.py:457

commit v6 on v5

--- a/solution.py
+++ b/solution.py
@@ -244,20 +244,28 @@
     ]
     for copy in arriving:
         copy.start()
+    step = 10
+    inside = jnp.concatenate([w_ref[b, LANES:] for b in range(3)], axis=0)
+    seam = jnp.concatenate([w_ref[b, :LANES] for b in range(3)], axis=0)
+
+    def part(refs, w, start):
+        x = jnp.concatenate([ref[start + b:start + b + step] for b in range(3) for ref in refs], axis=-1)
+        return jnp.dot(x.reshape(step * M, w.shape[0]), w, preferred_element_type=F32)
+
+    early = [part((own_ref, mate_ref), inside, start) for start in (0, step)]
     for copy in arriving:
         copy.wait()
     half = LW // 2
     skip = half - (LW - PACK)
-    x_ref[:half, :, :LANES] = jnp.concatenate([near_ref[:half, :, :C], far_ref[:half, :, :C]], axis=-1)
-    x_ref[half:, :, :LANES] = jnp.concatenate([near_ref[skip:, :, C:], far_ref[skip:, :, C:]], axis=-1)
-    step = 10
+    x_ref[:half] = jnp.concatenate([near_ref[:half, :, :C], far_ref[:half, :, :C]], axis=-1)
+    x_ref[half:] = jnp.concatenate([near_ref[skip:, :, C:], far_ref[skip:, :, C:]], axis=-1)
     w = w_ref[...].reshape(18 * C, 4 * C)
     copies = []
     for start in range(0, LV, step):
-        x = jnp.concatenate(
-            [ref[start + b:start + b + step] for b in range(3) for ref in (x_ref, own_ref, mate_ref)], axis=-1
-        )
-        v = jnp.dot(x.reshape(step * M, 18 * C), w, preferred_element_type=F32)
+        if start < HELD:
+            v = early[start // step] + part((x_ref,), seam, start)
+        else:
+            v = part((x_ref, own_ref, mate_ref), w, start)
         v = (v.reshape(step, M, 4 * C) * keep_ref[start:start + step]).astype(BF)
         if start < HELD:
             held_ref[start:start + step] = v

time: 119 us -> 119 us (level)
  no operation moved by 1% of the time
where the time goes in v6:
time: 119 us
  blocking collectives  79.6 us (67%)
  starting transfers between devices  17.2 us (14%)
  Pallas kernels  15.7 us (13%)
  waiting for transfers between devices  3.98 us (3%)
  local copies, waits for them, and re-layouts  1.79 us (2%)
    all_to_all x1, blocking collectives, local(): lax.all_to_all(windows, 'mem', split_axis=0, concat_axis=0, tiled=True)  32 us
    all_to_all x1, blocking collectives, local(): back = lax.all_to_all(mixed, 'mem', split_axis=0, concat_axis=0, tiled=True)  26 us
    all_to_all x1, blocking collectives, local(): attn = lax.all_to_all(attn, SPACE, split_axis=0, concat_axis=0, tiled=True)  12.4 us
    all_to_all x1, blocking collectives, local(): lax.all_to_all(summed(part, GROUPS), 'mem', split_axis=0, concat_axis=0,...  9.24 us
    all_to_all x1, starting transfers between devices, local(): part = lax.all_to_all(part, SPACE, split_axis=0, concat_axis=0, tiled=True)  9.14 us
    pallas_call x1, Pallas kernels, value_maps(): pl.pallas_call(values_kernel, in_specs=[hbm, hbm, vmem, vmem, vmem, vmem]...  4.4 us
    pallas_call x1, Pallas kernels, mix(): pl.pallas_call(mix_kernel, in_specs=[vmem, vmem, hbm, vmem, vmem], out_sh...  3.69 us
    all_to_all x1, waiting for transfers between devices, local(): part = lax.all_to_all(part, SPACE, split_axis=0, concat_axis=0, tiled=True)  3.28 us
  transfers between devices with their start and end apart: 4, of which 2 were waited for; matrix products, arithmetic and copies ran while one was open for 0% of the time, Pallas kernels for 8%

profile of v6, /device:TPU:1, one launch (start us, length us, event | category | flops | bytes accessed | tf_op | source)
XLA Modules:
  0.0 118.8 jit_solution(10190282955711167044)
XLA Ops:
  0.0 1.3 %copy.8 = bf16[8,2,64,384]{3,2,1,0:T(8,128)(2,1)S(1)} copy(bf16[8,2,64,384]{3,1,2,0:T(2,128)(2,1)} %bitcast.23) | data formatting | bytes 1572864 | tf_op jit(solution)/shard_map/transpose | solution.py:442
  1.3 0.5 shard_map.37
  1.7 0.0 copy-start.1
  1.8 32.0 %all_to_all.25 = bf16[8,52,8,128]{3,2,1,0:T(8,128)(2,1)S(1)} all-to-all(bf16[8,52,8,128]{3,2,1,0:T(8,128)(2,1)S(1)} %bitcast.18), channel_id=1, replica_groups=mesh['x'=4,'y'=4,'core'=2,'mem'=8] {'mem'}, dimensions={0} | all-to-all | bytes 1703936 | tf_op jit(solution)/shard_map/all_to_all | solution.py:444
  33.7 0.2 copy_bitcast_fusion.own_ref
  34.0 0.0 copy-start
  34.0 2.5 %collective-permute-start.1 = (bf16[52,64,128]{2,1,0:T(8,128)(2,1)S(1)}, bf16[52,64,128]{2,1,0:T(8,128)(2,1)S(1)}, u32[]{:S(2)}, u32[]{:S(2)}) collective-permute-start(bf16[52,64,128]{2,1,0:T(8,128)(2,1)S(1)} %copy_bitcast_fusion.own_ref), channel_id=1, source_target_pairs={{0,8},{8,0},{1,9},{9,1},{2,10},{10,2},{3,11},{11,3},{4,12},{12,4},... | collective-permute-start | bytes 2555912 | tf_op jit(solution)/shard_map/ppermute | solution.py:449
  36.5 0.0 copy-done.1
  36.5 0.1 copy.10
  36.7 0.2 shard_map.38
  36.9 3.1 %collective-permute-start = (bf16[28,64,128]{2,1,0:T(8,128)(2,1)S(1)}, bf16[28,64,128]{2,1,0:T(8,128)(2,1)S(1)}, u32[]{:S(2)}, u32[]{:S(2)}) collective-permute-start(bf16[28,64,128]{2,1,0:T(8,128)(2,1)S(1)} %shard_map.38), channel_id=1, source_target_pairs={{8,16},{24,32},{40,48},{56,64},{72,80},{88,96},{104,112},{120,128}... | collective-permute-start | bytes 1376264 | tf_op jit(solution)/shard_map/ppermute | solution.py:448
  40.0 0.2 or_select_fusion.keep_ref
  40.2 0.2 shard_map.42
  40.4 2.4 %collective-permute-start.2 = (bf16[28,64,128]{2,1,0:T(8,128)(2,1)S(1)}, bf16[28,64,128]{2,1,0:T(8,128)(2,1)}, u32[]{:S(2)}, u32[]{:S(2)}) collective-permute-start(bf16[28,64,128]{2,1,0:T(8,128)(2,1)S(1)} %shard_map.42), channel_id=1, source_target_pairs={{8,16},{24,32},{40,48},{56,64},{72,80},{88,96},{104,112},{120,128}... | collective-permute-start | bytes 1376264 | tf_op jit(solution)/shard_map/ppermute | solution.py:450
  42.9 0.0 copy-done
  42.9 0.8 shard_map.39
  43.7 0.0 collective-permute-done.1.mate_ref
  43.7 2.3 %shard_map.40 = (f32[64,512]{1,0:T(8,128)S(1)}, f32[48,64,128]{2,1,0:T(8,128)S(1)}) custom-call(bf16[52,64,128]{2,1,0:T(8,128)(2,1)S(1)} %collective-permute-done.1.mate_ref, bf16[52,64,128]{2,1,0:T(8,128)(2,1)S(1)} %copy_bitcast_fusion.own_ref, bf16[3,256,256]{2,1,0:T(8,128)(2,1)S(1)} %get-tuple-element.22.w_ref), custom_call_target="tpu_custom_call" | custom-call | flops 3000000000 | bytes 3000000 | tf_op jit(solution)/shard_map/pallas_call | solution.py:220
  46.0 0.7 collective-permute-done.near_ref
  46.7 2.1 %shard_map.41 = (f32[32,8,128]{2,1,0:T(8,128)}, bf16[28,64,128]{2,1,0:T(8,128)(2,1)}) custom-call(bf16[28,64,128]{2,1,0:T(8,128)(2,1)S(1)} %collective-permute-done.near_ref, f32[48,64,128]{2,1,0:T(8,128)S(1)} %get-tuple-element.23.late_ref, f32[64,512]{1,0:T(8,128)S(1)} %get-tuple-element.24.first_ref, bf16[384,256]{1,0:T(8,128)(2,1)S(1)} %get-tuple-element.25.w_ref), custom_call_target="tpu_custom_call" | custom-call | flops 2000000000 | bytes 3000000 | tf_op jit(solution)/shard_map/pallas_call | solution.py:230
  48.8 9.1 %all-to-all-start.1 = ((f32[32,8,128]{2,1,0:T(8,128)}), f32[32,8,128]{2,1,0:T(8,128)S(1)}, u32[]{:S(2)}, u32[]{:S(2)}) async-start(f32[32,8,128]{2,1,0:T(8,128)} %get-tuple-element.26), calls=%async_computation.1 | async-start | bytes 262144 | tf_op jit(solution)/shard_map/all_to_all | solution.py:465
  57.9 0.0 collective-permute-done.2.far_in
  57.9 4.4 %shard_map.43 = (bf16[20,64,256]{2,1,0:T(8,128)(2,1)S(1)}, bf16[30,64,256]{2,1,0:T(8,128)(2,1)}) custom-call(bf16[28,64,128]{2,1,0:T(8,128)(2,1)} %get-tuple-element.27.near_in, bf16[28,64,128]{2,1,0:T(8,128)(2,1)} %collective-permute-done.2.far_in, bf16[52,64,128]{2,1,0:T(8,128)(2,1)S(1)} %copy_bitcast_fusion.own_ref, ...), custom_call_target="tpu_custom_call" | custom-call | flops 2000000000 | bytes 4000000 | tf_op jit(solution)/shard_map/pallas_call | solution.py:284
  62.3 3.3 %all-to-all-done.1.parts_ref = f32[32,8,128]{2,1,0:T(8,128)S(1)} async-done(((f32[32,8,128]{2,1,0:T(8,128)}), f32[32,8,128]{2,1,0:T(8,128)S(1)}, u32[]{:S(2)}, u32[]{:S(2)}) %all-to-all-start.1) | async-done | bytes 131104 | tf_op jit(solution)/shard_map/all_to_all | solution.py:465
  65.7 9.2 %all_to_all.26.parts_ref = f32[8,8,128]{2,1,0:T(8,128)S(1)} all-to-all(f32[8,8,128]{2,1,0:T(8,128)S(1)} %shard_map.44), channel_id=1, replica_groups=mesh['x'=4,'y'=4,'core'=2,'mem'=8] {'mem'}, dimensions={0} | all-to-all | bytes 65536 | tf_op jit(solution)/shard_map/all_to_all | solution.py:468
  74.9 0.2 shard_map.45
  75.1 12.4 %all_to_all.27.attn_ref = bf16[32,8,128]{2,1,0:T(8,128)(2,1)S(1)} all-to-all(bf16[32,8,128]{2,1,0:T(8,128)(2,1)S(1)} %shard_map.45), channel_id=1, replica_groups=mesh['x'=4,'y'=4,'core'=2,'mem'=8] {'x','y','core'}, dimensions={0} | all-to-all | bytes 131072 | tf_op jit(solution)/shard_map/all_to_all | solution.py:470
  87.5 3.7 %shard_map.46 = bf16[48,64,128]{2,1,0:T(8,128)(2,1)S(1)} custom-call(bf16[32,8,128]{2,1,0:T(8,128)(2,1)S(1)} %all_to_all.27.attn_ref, bf16[20,64,256]{2,1,0:T(8,128)(2,1)S(1)} %get-tuple-element.32.held_ref, bf16[30,64,256]{2,1,0:T(8,128)(2,1)} %get-tuple-element.33.v_in, bf16[52,64,128]{2,1,0:T(8,128)(2,1)S(1)} %copy_bitcast_fusion.own_ref, ...), custom_call_target="tpu_custom_call" | custom-call | flops 4000000000 | bytes 4000000 | tf_op jit(solution)/shard_map/pallas_call | solution.py:336
  91.2 0.1 copy_bitcast_fusion.1
  91.4 26.0 %all_to_all.28 = bf16[8,48,8,128]{3,2,1,0:T(8,128)(2,1)S(1)} all-to-all(bf16[8,48,8,128]{3,2,1,0:T(8,128)(2,1)S(1)} %copy_bitcast_fusion.1), channel_id=1, replica_groups=mesh['x'=4,'y'=4,'core'=2,'mem'=8] {'mem'}, dimensions={0} | all-to-all | bytes 1572864 | tf_op jit(solution)/shard_map/all_to_all | solution.py:473
  117.3 1.4 %shard_map.47 = bf16[8,64,2,384]{3,2,1,0:T(2,128)(2,1)} custom-call(bf16[8,384,128]{2,1,0:T(8,128)(2,1)S(1)} %bitcast.19), custom_call_target="tpu_custom_call" | custom-call | bytes 1600000 | tf_op jit(solution)/shard_map/pallas_call | solution.py:420
  (4 shorter events, 0.1 us)
Async XLA Ops:
  1.7 34.8 %copy-start.1 = (bf16[9,64,64]{2,1,0:T(8,128)(2,1)S(1)}, bf16[9,64,64]{2,1,0:T(8,128)(2,1)}, u32[]{:S(2)}) copy-start(bf16[9,64,64]{2,1,0:T(8,128)(2,1)} %param.5) | copy-start | bytes 221188
  34.0 8.9 %copy-start = (bf16[9,192,64]{1,2,0:T(8,128)(2,1)S(1)}, bf16[9,192,64]{1,2,0:T(8,128)(2,1)}, u32[]{:S(2)}) copy-start(bf16[9,192,64]{1,2,0:T(8,128)(2,1)} %param.4) | copy-start | bytes 663556
  34.0 9.7 %collective-permute-start.1 = (bf16[52,64,128]{2,1,0:T(8,128)(2,1)S(1)}, bf16[52,64,128]{2,1,0:T(8,128)(2,1)S(1)}, u32[]{:S(2)}, u32[]{:S(2)}) collective-permute-start(bf16[52,64,128]{2,1,0:T(8,128)(2,1)S(1)} %copy_bitcast_fusion.own_ref), channel_id=1, source_target_pairs={{0,8},{8,0},{1,9},{9,1},{2,10},{10,2},{3,11},{11,3},{4,12},{12,4},... | collective-permute-start | bytes 2555912 | tf_op jit(solution)/shard_map/ppermute | solution.py:449
  36.9 9.8 %collective-permute-start = (bf16[28,64,128]{2,1,0:T(8,128)(2,1)S(1)}, bf16[28,64,128]{2,1,0:T(8,128)(2,1)S(1)}, u32[]{:S(2)}, u32[]{:S(2)}) collective-permute-start(bf16[28,64,128]{2,1,0:T(8,128)(2,1)S(1)} %shard_map.38), channel_id=1, source_target_pairs={{8,16},{24,32},{40,48},{56,64},{72,80},{88,96},{104,112},{120,128}... | collective-permute-start | bytes 1376264 | tf_op jit(solution)/shard_map/ppermute | solution.py:448
  40.4 17.5 %collective-permute-start.2 = (bf16[28,64,128]{2,1,0:T(8,128)(2,1)S(1)}, bf16[28,64,128]{2,1,0:T(8,128)(2,1)}, u32[]{:S(2)}, u32[]{:S(2)}) collective-permute-start(bf16[28,64,128]{2,1,0:T(8,128)(2,1)S(1)} %shard_map.42), channel_id=1, source_target_pairs={{8,16},{24,32},{40,48},{56,64},{72,80},{88,96},{104,112},{120,128}... | collective-permute-start | bytes 1376264 | tf_op jit(solution)/shard_map/ppermute | solution.py:450
  48.8 16.9 %all-to-all-start.1 = ((f32[32,8,128]{2,1,0:T(8,128)}), f32[32,8,128]{2,1,0:T(8,128)S(1)}, u32[]{:S(2)}, u32[]{:S(2)}) async-start(f32[32,8,128]{2,1,0:T(8,128)} %get-tuple-element.26), calls=%async_computation.1 | async-start | bytes 262144 | tf_op jit(solution)/shard_map/all_to_all | solution.py:465

commit v7 on v5

--- a/solution.py
+++ b/solution.py
@@ -26,7 +26,7 @@
 SPACE = ("x", "y", "core")
 BF = jnp.bfloat16
 F32 = jnp.float32
-VMEM_LIMIT = 24 * 1024 * 1024
+VMEM_LIMIT = 16 * 1024 * 1024
 
 
 def place_weights_kernel(core_ref, w_ref, wo_ref, qk_ref, near_ref, v_ref, o_ref, plain_ref):

time: 119 us -> 119 us (level)
  no operation moved by 1% of the time
where the time goes in v7:
time: 119 us
  blocking collectives  79.7 us (67%)
  starting transfers between devices  17.2 us (14%)
  Pallas kernels  15.8 us (13%)
  waiting for transfers between devices  3.95 us (3%)
  local copies, waits for them, and re-layouts  1.79 us (2%)
    all_to_all x1, blocking collectives, local(): lax.all_to_all(windows, 'mem', split_axis=0, concat_axis=0, tiled=True)  32 us
    all_to_all x1, blocking collectives, local(): back = lax.all_to_all(mixed, 'mem', split_axis=0, concat_axis=0, tiled=True)  26 us
    all_to_all x1, blocking collectives, local(): attn = lax.all_to_all(attn, SPACE, split_axis=0, concat_axis=0, tiled=True)  12.5 us
    all_to_all x1, blocking collectives, local(): lax.all_to_all(summed(part, GROUPS), 'mem', split_axis=0, concat_axis=0,...  9.24 us
    all_to_all x1, starting transfers between devices, local(): part = lax.all_to_all(part, SPACE, split_axis=0, concat_axis=0, tiled=True)  9.14 us
    pallas_call x1, Pallas kernels, value_maps(): pl.pallas_call(values_kernel, in_specs=[hbm, hbm, vmem, vmem, vmem, vmem]...  4.43 us
    pallas_call x1, Pallas kernels, mix(): pl.pallas_call(mix_kernel, in_specs=[vmem, vmem, hbm, vmem, vmem], out_sh...  3.69 us
    all_to_all x1, waiting for transfers between devices, local(): part = lax.all_to_all(part, SPACE, split_axis=0, concat_axis=0, tiled=True)  3.25 us
  transfers between devices with their start and end apart: 4, of which 2 were waited for; matrix products, arithmetic and copies ran while one was open for 0% of the time, Pallas kernels for 8%

profile of v7, /device:TPU:1, one launch (start us, length us, event | category | flops | bytes accessed | tf_op | source)
XLA Modules:
  0.0 118.8 jit_solution(14821124778329576490)
XLA Ops:
  0.0 1.3 %copy.8 = bf16[8,2,64,384]{3,2,1,0:T(8,128)(2,1)S(1)} copy(bf16[8,2,64,384]{3,1,2,0:T(2,128)(2,1)} %bitcast.23) | data formatting | bytes 1572864 | tf_op jit(solution)/shard_map/transpose | solution.py:434
  1.3 0.5 shard_map.37
  1.7 0.0 copy-start.1
  1.8 32.0 %all_to_all.25 = bf16[8,52,8,128]{3,2,1,0:T(8,128)(2,1)S(1)} all-to-all(bf16[8,52,8,128]{3,2,1,0:T(8,128)(2,1)S(1)} %bitcast.18), channel_id=1, replica_groups=mesh['x'=4,'y'=4,'core'=2,'mem'=8] {'mem'}, dimensions={0} | all-to-all | bytes 1703936 | tf_op jit(solution)/shard_map/all_to_all | solution.py:436
  33.7 0.2 copy_bitcast_fusion.own_ref
  34.0 0.0 copy-start
  34.0 2.5 %collective-permute-start.1 = (bf16[52,64,128]{2,1,0:T(8,128)(2,1)S(1)}, bf16[52,64,128]{2,1,0:T(8,128)(2,1)S(1)}, u32[]{:S(2)}, u32[]{:S(2)}) collective-permute-start(bf16[52,64,128]{2,1,0:T(8,128)(2,1)S(1)} %copy_bitcast_fusion.own_ref), channel_id=1, source_target_pairs={{0,8},{8,0},{1,9},{9,1},{2,10},{10,2},{3,11},{11,3},{4,12},{12,4},... | collective-permute-start | bytes 2555912 | tf_op jit(solution)/shard_map/ppermute | solution.py:441
  36.5 0.0 copy-done.1
  36.5 0.1 copy.10
  36.7 0.2 shard_map.38
  36.9 3.1 %collective-permute-start = (bf16[28,64,128]{2,1,0:T(8,128)(2,1)S(1)}, bf16[28,64,128]{2,1,0:T(8,128)(2,1)S(1)}, u32[]{:S(2)}, u32[]{:S(2)}) collective-permute-start(bf16[28,64,128]{2,1,0:T(8,128)(2,1)S(1)} %shard_map.38), channel_id=1, source_target_pairs={{8,16},{24,32},{40,48},{56,64},{72,80},{88,96},{104,112},{120,128}... | collective-permute-start | bytes 1376264 | tf_op jit(solution)/shard_map/ppermute | solution.py:440
  40.0 0.2 or_select_fusion.keep_ref
  40.2 0.2 shard_map.42
  40.4 2.4 %collective-permute-start.2 = (bf16[28,64,128]{2,1,0:T(8,128)(2,1)S(1)}, bf16[28,64,128]{2,1,0:T(8,128)(2,1)}, u32[]{:S(2)}, u32[]{:S(2)}) collective-permute-start(bf16[28,64,128]{2,1,0:T(8,128)(2,1)S(1)} %shard_map.42), channel_id=1, source_target_pairs={{8,16},{24,32},{40,48},{56,64},{72,80},{88,96},{104,112},{120,128}... | collective-permute-start | bytes 1376264 | tf_op jit(solution)/shard_map/ppermute | solution.py:442
  42.9 0.0 copy-done
  42.9 0.8 shard_map.39
  43.7 0.0 collective-permute-done.1.mate_ref
  43.7 2.3 %shard_map.40 = (f32[64,512]{1,0:T(8,128)S(1)}, f32[48,64,128]{2,1,0:T(8,128)S(1)}) custom-call(bf16[52,64,128]{2,1,0:T(8,128)(2,1)S(1)} %collective-permute-done.1.mate_ref, bf16[52,64,128]{2,1,0:T(8,128)(2,1)S(1)} %copy_bitcast_fusion.own_ref, bf16[3,256,256]{2,1,0:T(8,128)(2,1)S(1)} %get-tuple-element.22.w_ref), custom_call_target="tpu_custom_call" | custom-call | flops 3000000000 | bytes 3000000 | tf_op jit(solution)/shard_map/pallas_call | solution.py:220
  46.0 0.7 collective-permute-done.near_ref
  46.7 2.1 %shard_map.41 = (f32[32,8,128]{2,1,0:T(8,128)}, bf16[28,64,128]{2,1,0:T(8,128)(2,1)}) custom-call(bf16[28,64,128]{2,1,0:T(8,128)(2,1)S(1)} %collective-permute-done.near_ref, f32[48,64,128]{2,1,0:T(8,128)S(1)} %get-tuple-element.23.late_ref, f32[64,512]{1,0:T(8,128)S(1)} %get-tuple-element.24.first_ref, bf16[384,256]{1,0:T(8,128)(2,1)S(1)} %get-tuple-element.25.w_ref), custom_call_target="tpu_custom_call" | custom-call | flops 2000000000 | bytes 3000000 | tf_op jit(solution)/shard_map/pallas_call | solution.py:230
  48.8 9.1 %all-to-all-start.1 = ((f32[32,8,128]{2,1,0:T(8,128)}), f32[32,8,128]{2,1,0:T(8,128)S(1)}, u32[]{:S(2)}, u32[]{:S(2)}) async-start(f32[32,8,128]{2,1,0:T(8,128)} %get-tuple-element.26), calls=%async_computation.1 | async-start | bytes 262144 | tf_op jit(solution)/shard_map/all_to_all | solution.py:457
  57.9 0.0 collective-permute-done.2.far_in
  57.9 4.4 %shard_map.43 = (bf16[20,64,256]{2,1,0:T(8,128)(2,1)S(1)}, bf16[30,64,256]{2,1,0:T(8,128)(2,1)}) custom-call(bf16[28,64,128]{2,1,0:T(8,128)(2,1)} %get-tuple-element.27.near_in, bf16[28,64,128]{2,1,0:T(8,128)(2,1)} %collective-permute-done.2.far_in, bf16[52,64,128]{2,1,0:T(8,128)(2,1)S(1)} %copy_bitcast_fusion.own_ref, ...), custom_call_target="tpu_custom_call" | custom-call | flops 2000000000 | bytes 4000000 | tf_op jit(solution)/shard_map/pallas_call | solution.py:276
  62.4 3.3 %all-to-all-done.1.parts_ref = f32[32,8,128]{2,1,0:T(8,128)S(1)} async-done(((f32[32,8,128]{2,1,0:T(8,128)}), f32[32,8,128]{2,1,0:T(8,128)S(1)}, u32[]{:S(2)}, u32[]{:S(2)}) %all-to-all-start.1) | async-done | bytes 131104 | tf_op jit(solution)/shard_map/all_to_all | solution.py:457
  65.7 9.2 %all_to_all.26.parts_ref = f32[8,8,128]{2,1,0:T(8,128)S(1)} all-to-all(f32[8,8,128]{2,1,0:T(8,128)S(1)} %shard_map.44), channel_id=1, replica_groups=mesh['x'=4,'y'=4,'core'=2,'mem'=8] {'mem'}, dimensions={0} | all-to-all | bytes 65536 | tf_op jit(solution)/shard_map/all_to_all | solution.py:460
  74.9 0.2 shard_map.45
  75.1 12.5 %all_to_all.27.attn_ref = bf16[32,8,128]{2,1,0:T(8,128)(2,1)S(1)} all-to-all(bf16[32,8,128]{2,1,0:T(8,128)(2,1)S(1)} %shard_map.45), channel_id=1, replica_groups=mesh['x'=4,'y'=4,'core'=2,'mem'=8] {'x','y','core'}, dimensions={0} | all-to-all | bytes 131072 | tf_op jit(solution)/shard_map/all_to_all | solution.py:462
  87.5 3.7 %shard_map.46 = bf16[48,64,128]{2,1,0:T(8,128)(2,1)S(1)} custom-call(bf16[32,8,128]{2,1,0:T(8,128)(2,1)S(1)} %all_to_all.27.attn_ref, bf16[20,64,256]{2,1,0:T(8,128)(2,1)S(1)} %get-tuple-element.32.held_ref, bf16[30,64,256]{2,1,0:T(8,128)(2,1)} %get-tuple-element.33.v_in, bf16[52,64,128]{2,1,0:T(8,128)(2,1)S(1)} %copy_bitcast_fusion.own_ref, ...), custom_call_target="tpu_custom_call" | custom-call | flops 4000000000 | bytes 4000000 | tf_op jit(solution)/shard_map/pallas_call | solution.py:328
  91.2 0.1 copy_bitcast_fusion.1
  91.4 26.0 %all_to_all.28 = bf16[8,48,8,128]{3,2,1,0:T(8,128)(2,1)S(1)} all-to-all(bf16[8,48,8,128]{3,2,1,0:T(8,128)(2,1)S(1)} %copy_bitcast_fusion.1), channel_id=1, replica_groups=mesh['x'=4,'y'=4,'core'=2,'mem'=8] {'mem'}, dimensions={0} | all-to-all | bytes 1572864 | tf_op jit(solution)/shard_map/all_to_all | solution.py:465
  117.4 1.4 %shard_map.47 = bf16[8,64,2,384]{3,2,1,0:T(2,128)(2,1)} custom-call(bf16[8,384,128]{2,1,0:T(8,128)(2,1)S(1)} %bitcast.19), custom_call_target="tpu_custom_call" | custom-call | bytes 1600000 | tf_op jit(solution)/shard_map/pallas_call | solution.py:412
  (4 shorter events, 0.1 us)
Async XLA Ops:
  1.7 34.8 %copy-start.1 = (bf16[9,64,64]{2,1,0:T(8,128)(2,1)S(1)}, bf16[9,64,64]{2,1,0:T(8,128)(2,1)}, u32[]{:S(2)}) copy-start(bf16[9,64,64]{2,1,0:T(8,128)(2,1)} %param.5) | copy-start | bytes 221188
  34.0 8.9 %copy-start = (bf16[9,192,64]{1,2,0:T(8,128)(2,1)S(1)}, bf16[9,192,64]{1,2,0:T(8,128)(2,1)}, u32[]{:S(2)}) copy-start(bf16[9,192,64]{1,2,0:T(8,128)(2,1)} %param.4) | copy-start | bytes 663556
  34.0 9.7 %collective-permute-start.1 = (bf16[52,64,128]{2,1,0:T(8,128)(2,1)S(1)}, bf16[52,64,128]{2,1,0:T(8,128)(2,1)S(1)}, u32[]{:S(2)}, u32[]{:S(2)}) collective-permute-start(bf16[52,64,128]{2,1,0:T(8,128)(2,1)S(1)} %copy_bitcast_fusion.own_ref), channel_id=1, source_target_pairs={{0,8},{8,0},{1,9},{9,1},{2,10},{10,2},{3,11},{11,3},{4,12},{12,4},... | collective-permute-start | bytes 2555912 | tf_op jit(solution)/shard_map/ppermute | solution.py:441
  36.9 9.8 %collective-permute-start = (bf16[28,64,128]{2,1,0:T(8,128)(2,1)S(1)}, bf16[28,64,128]{2,1,0:T(8,128)(2,1)S(1)}, u32[]{:S(2)}, u32[]{:S(2)}) collective-permute-start(bf16[28,64,128]{2,1,0:T(8,128)(2,1)S(1)} %shard_map.38), channel_id=1, source_target_pairs={{8,16},{24,32},{40,48},{56,64},{72,80},{88,96},{104,112},{120,128}... | collective-permute-start | bytes 1376264 | tf_op jit(solution)/shard_map/ppermute | solution.py:440
  40.4 17.5 %collective-permute-start.2 = (bf16[28,64,128]{2,1,0:T(8,128)(2,1)S(1)}, bf16[28,64,128]{2,1,0:T(8,128)(2,1)}, u32[]{:S(2)}, u32[]{:S(2)}) collective-permute-start(bf16[28,64,128]{2,1,0:T(8,128)(2,1)S(1)} %shard_map.42), channel_id=1, source_target_pairs={{8,16},{24,32},{40,48},{56,64},{72,80},{88,96},{104,112},{120,128}... | collective-permute-start | bytes 1376264 | tf_op jit(solution)/shard_map/ppermute | solution.py:442
  48.8 16.9 %all-to-all-start.1 = ((f32[32,8,128]{2,1,0:T(8,128)}), f32[32,8,128]{2,1,0:T(8,128)S(1)}, u32[]{:S(2)}, u32[]{:S(2)}) async-start(f32[32,8,128]{2,1,0:T(8,128)} %get-tuple-element.26), calls=%async_computation.1 | async-start | bytes 262144 | tf_op jit(solution)/shard_map/all_to_all | solution.py:457
